TPU v7x, 256 devices: a whole 4x4x8 slice. The times are simulated.
256 devices in a mesh: fx: 16 (over z_hi, x), fy: 16 (over z_lo, y, core).
Axes of the slice: x: 4, y: 4, z: 8 (z_hi: 4, z_lo: 2; z = z_hi * 2 + z_lo), core: 2. Of those that a mesh axis runs over, the one named last changes fastest.
Arguments:
- features: bfloat16 [12, 256, 256, 128], P(None, 'fx', 'fy'), may hold values from -6 to 6
- weight: bfloat16 [3, 3, 128, 128], replicated, may hold values from -0.1875 to 0.1875
- out_bias: float32 [128], replicated, may hold values from -3 to 3
- cotangent: bfloat16 [12, 256, 256, 128], P(None, 'fx', 'fy'), may hold values from -6 to 6
- seam_face: int32 [12, 4], replicated, may hold values from 0 to 11, as said below
- seam_edge: int32 [12, 4], replicated, may hold values from 0 to 3, as said below
- seam_flip: int32 [12, 4], replicated, may hold values from 0 to 1, as said below
Outputs:
- activated: bfloat16 [12, 256, 256, 128], P(None, 'fx', 'fy')
- gradient: bfloat16 [12, 256, 256, 128], P(None, 'fx', 'fy')
Inputs may be any that keep to these rules, and one draw needn't show every extreme that they name: seam_face and seam_edge pair all 48 edges two by two in an arbitrary pairing (two edges of one face may be glued): the edge glued to edge (seam_face[f, e], seam_edge[f, e]) is (f, e) again, and no edge is glued to itself. `seam_edge`: edge codes: 0 row 0, 1 last row, 2 column 0, 3 last column. `seam_flip`: both edges of a glued pair carry the same value.
All inputs are finite; a program needn't handle non-finite values.
Results may differ from a plain program's by a relative error of at most 0.0049.
Values may be sent and summed in bfloat16 or wider, within the bound.
A program may use at most 64 MiB of HBM per device.

v0:
```python
import jax
import jax.numpy as jnp
from jax import lax
from jax.sharding import PartitionSpec as P


def spread_2(block, axis, source):
    block = jnp.where(lax.axis_index(axis) == source, block, jnp.zeros_like(block))
    return lax.psum(block, axis)


def extended(cells, sides, width):
    for axis, dim in sides:
        count = lax.axis_size(axis)
        ends = count - 1
        head = lax.slice_in_dim(cells, 0, width, axis=dim)
        tail = lax.slice_in_dim(cells, cells.shape[dim] - width, cells.shape[dim], axis=dim)
        cells = jnp.concatenate(
            [
                lax.ppermute(tail, axis, [(i, (i + 1) % count) for i in range(ends)]),
                cells,
                lax.ppermute(head, axis, [((i + 1) % count, i) for i in range(ends)]),
            ],
            axis=dim,
        )
    return cells


def passed_along(value, axis, steps):
    count = lax.axis_size(axis)
    initial, last = (max(0, -steps), min(count, count - steps))
    return lax.ppermute(value, axis, [(source, source + steps) for source in range(initial, last)])


def silu_slope(value):
    sigma = jax.nn.sigmoid(value)
    return sigma * (1.0 + value * (1.0 - sigma))


def tap_sum(source, weight, row_total, col_total, adjoint):
    summed = None
    for tap_row in range(3):
        for tap_col in range(3):
            if adjoint:
                row_from = 2 - tap_row
                col_from = 2 - tap_col
                einsum_form = "fijd,cd->fijc"
            else:
                row_from = tap_row
                col_from = tap_col
                einsum_form = "fijc,cd->fijd"
            window = source[:, row_from : row_from + row_total, col_from : col_from + col_total]
            product = jnp.einsum(
                einsum_form, window, weight[tap_row, tap_col], preferred_element_type=jnp.float32
            )
            summed = product if summed is None else summed + product
    return summed


def oriented(edge_lines, seam_face, seam_edge, seam_flip, positions):
    side_len = edge_lines.shape[2]
    turned = jnp.where(
        seam_flip[:, :, None] == 1,
        side_len - 1 - positions[None, None, :],
        positions[None, None, :],
    )
    return edge_lines[seam_face[:, :, None], seam_edge[:, :, None], turned]


def corner_values(edge_lines, seam_face, seam_edge, seam_flip):
    side_len = edge_lines.shape[2]
    end_values = oriented(
        edge_lines, seam_face, seam_edge, seam_flip, jnp.array([0, side_len - 1], jnp.int32)
    )
    end_values = end_values.astype(jnp.float32)
    north_west = (0.5 * (end_values[:, 0, 0] + end_values[:, 2, 0])).astype(jnp.bfloat16)
    north_east = (0.5 * (end_values[:, 0, 1] + end_values[:, 3, 0])).astype(jnp.bfloat16)
    south_west = (0.5 * (end_values[:, 1, 0] + end_values[:, 2, 1])).astype(jnp.bfloat16)
    south_east = (0.5 * (end_values[:, 1, 1] + end_values[:, 3, 1])).astype(jnp.bfloat16)
    return (north_west, north_east, south_west, south_east)


def seam_segment(edge_lines, seam_face, seam_edge, seam_flip, spot_list, first_pair, last_pair):
    side_len = edge_lines.shape[2]
    values = oriented(
        edge_lines, seam_face, seam_edge, seam_flip, jnp.clip(spot_list, 0, side_len - 1)
    )
    values = jnp.where(spot_list[None, None, :, None] < 0, first_pair[:, :, None], values)
    return jnp.where(spot_list[None, None, :, None] >= side_len, last_pair[:, :, None], values)


def split_ends(cycle_line, first_on, last_on):
    inner = cycle_line[:, 1:-1]
    inner = inner.at[:, 0].add(jnp.where(first_on, 0.5 * cycle_line[:, 0], 0.0))
    inner = inner.at[:, -1].add(jnp.where(last_on, 0.5 * cycle_line[:, -1], 0.0))
    return inner


def shards(features, weight, out_bias, cotangent, seam_face, seam_edge, seam_flip):
    face_count, patch_rows, patch_cols, channels = features.shape
    row_count = lax.axis_size("fx")
    col_count = lax.axis_size("fy")
    row_index = lax.axis_index("fx")
    col_index = lax.axis_index("fy")
    north_strip = features[:, 0]
    south_strip = features[:, -1]
    west_strip = features[:, :, 0]
    east_strip = features[:, :, -1]
    north_line, south_line = (
        lax.all_gather(north_strip, "fy", axis=1, tiled=True),
        lax.all_gather(south_strip, "fy", axis=1, tiled=True),
    )
    west_line, east_line = (
        lax.all_gather(west_strip, "fx", axis=1, tiled=True),
        lax.all_gather(east_strip, "fx", axis=1, tiled=True),
    )
    north_line = spread_2(north_line, "fx", 0)
    south_line = spread_2(south_line, "fx", row_count - 1)
    west_line = spread_2(west_line, "fy", 0)
    east_line = spread_2(east_line, "fy", col_count - 1)
    edge_lines = jnp.stack([north_line, south_line, west_line, east_line], axis=1)
    north_west, north_east, south_west, south_east = corner_values(
        edge_lines, seam_face, seam_edge, seam_flip
    )
    col_spots = col_index * patch_cols - 1 + jnp.arange(patch_cols + 2, dtype=jnp.int32)
    row_spots = row_index * patch_rows - 1 + jnp.arange(patch_rows + 2, dtype=jnp.int32)
    row_seams = seam_segment(
        edge_lines,
        seam_face[:, 0:2],
        seam_edge[:, 0:2],
        seam_flip[:, 0:2],
        col_spots,
        jnp.stack([north_west, south_west], 1),
        jnp.stack([north_east, south_east], 1),
    )
    col_seams = seam_segment(
        edge_lines,
        seam_face[:, 2:4],
        seam_edge[:, 2:4],
        seam_flip[:, 2:4],
        row_spots,
        jnp.stack([north_west, north_east], 1),
        jnp.stack([south_west, south_east], 1),
    )
    top_on = row_index == 0
    bottom_on = row_index == row_count - 1
    left_on = col_index == 0
    right_on = col_index == col_count - 1
    padded = extended(features, (("fx", 1), ("fy", 2)), 1)
    padded = padded.at[:, 0].set(jnp.where(top_on, row_seams[:, 0], padded[:, 0]))
    padded = padded.at[:, -1].set(jnp.where(bottom_on, row_seams[:, 1], padded[:, -1]))
    padded = padded.at[:, :, 0].set(jnp.where(left_on, col_seams[:, 0], padded[:, :, 0]))
    padded = padded.at[:, :, -1].set(jnp.where(right_on, col_seams[:, 1], padded[:, :, -1]))
    preact = tap_sum(padded, weight, patch_rows, patch_cols, False) + out_bias
    activated = jax.nn.silu(preact).astype(jnp.bfloat16)
    slope = (cotangent.astype(jnp.float32) * silu_slope(preact)).astype(jnp.bfloat16)
    grad_padded = jnp.pad(slope, ((0, 0), (2, 2), (2, 2), (0, 0)))
    spread = tap_sum(grad_padded, weight, patch_rows + 2, patch_cols + 2, True)
    from_right = passed_along(spread[:, :, 0].astype(jnp.bfloat16), "fy", -1).astype(jnp.float32)
    from_left = passed_along(spread[:, :, -1].astype(jnp.bfloat16), "fy", 1).astype(jnp.float32)
    spread = spread.at[:, :, -2].add(from_right).at[:, :, 1].add(from_left)
    from_below = passed_along(spread[:, 0].astype(jnp.bfloat16), "fx", -1).astype(jnp.float32)
    from_above = passed_along(spread[:, -1].astype(jnp.bfloat16), "fx", 1).astype(jnp.float32)
    spread = spread.at[:, -2].add(from_below).at[:, 1].add(from_above)
    cycle_north = jnp.where(top_on, split_ends(spread[:, 0], left_on, right_on), 0.0)
    cycle_south = jnp.where(bottom_on, split_ends(spread[:, -1], left_on, right_on), 0.0)
    cycle_west = jnp.where(left_on, split_ends(spread[:, :, 0], top_on, bottom_on), 0.0)
    cycle_east = jnp.where(right_on, split_ends(spread[:, :, -1], top_on, bottom_on), 0.0)
    row_cycles = jnp.stack([cycle_north, cycle_south], 1).astype(jnp.bfloat16)
    col_cycles = jnp.stack([cycle_west, cycle_east], 1).astype(jnp.bfloat16)
    row_across = lax.psum(row_cycles, "fx").astype(jnp.float32).astype(jnp.bfloat16)
    row_whole = lax.all_gather(row_across, "fy", axis=2, tiled=True)
    col_across = lax.psum(col_cycles, "fy").astype(jnp.float32).astype(jnp.bfloat16)
    col_whole = lax.all_gather(col_across, "fx", axis=2, tiled=True)
    cycle_lines = jnp.concatenate([row_whole, col_whole], 1)
    own_cols = col_index * patch_cols + jnp.arange(patch_cols, dtype=jnp.int32)
    own_rows = row_index * patch_rows + jnp.arange(patch_rows, dtype=jnp.int32)
    row_back = oriented(
        cycle_lines, seam_face[:, 0:2], seam_edge[:, 0:2], seam_flip[:, 0:2], own_cols
    ).astype(jnp.float32)
    col_back = oriented(
        cycle_lines, seam_face[:, 2:4], seam_edge[:, 2:4], seam_flip[:, 2:4], own_rows
    ).astype(jnp.float32)
    inner = spread[:, 1:-1, 1:-1]
    inner = inner.at[:, 0].add(jnp.where(top_on, row_back[:, 0], 0.0))
    inner = inner.at[:, -1].add(jnp.where(bottom_on, row_back[:, 1], 0.0))
    inner = inner.at[:, :, 0].add(jnp.where(left_on, col_back[:, 0], 0.0))
    inner = inner.at[:, :, -1].add(jnp.where(right_on, col_back[:, 1], 0.0))
    return (activated, inner.astype(jnp.bfloat16))


def solution(mesh):
    in_specs = (P(None, "fx", "fy", None), P(), P(), P(None, "fx", "fy", None), P(), P(), P())
    out_specs = (P(None, "fx", "fy", None), P(None, "fx", "fy", None))
    return jax.shard_map(shards, mesh=mesh, in_specs=in_specs, out_specs=out_specs, check_vma=False)
```

profile of v0, /device:TPU:57, one launch (start us, length us, event | category | flops | bytes accessed | tf_op | source)
XLA Modules:
  0.0 890.0 jit_solution(8440976796246208917)
XLA Ops:
  7.2 1.3 fusion.149
  8.5 44.5 %all-gather.3 = bf16[12,256,1,128]{3,1,0,2:T(8,128)(2,1)S(1)} all-gather(bf16[12,16,1,128]{3,1,0,2:T(8,128)(2,1)S(1)} %copy.159), channel_id=5, replica_groups=mesh['fx'=16,'fy'=16] {'fx'}, dimensions={1}, use_global_device_ids=true | all-gather | bytes 835584 | tf_op jit(solution)/shard_map/all_gather | solution.py:115
  53.0 37.8 %all-gather.2 = bf16[12,256,1,128]{3,1,0,2:T(8,128)(2,1)S(1)} all-gather(bf16[12,16,1,128]{3,1,0,2:T(8,128)(2,1)S(1)} %copy.158), channel_id=4, replica_groups=mesh['fx'=16,'fy'=16] {'fx'}, dimensions={1}, use_global_device_ids=true | all-gather | bytes 835584 | tf_op jit(solution)/shard_map/all_gather | solution.py:114
  90.8 0.9 select_bitcast_fusion
  91.7 0.9 select_bitcast_fusion.1
  93.2 1.3 collective-permute-start.1
  94.5 4.3 collective-permute-start
  98.8 32.0 %all-gather = bf16[12,1,256,128]{3,2,1,0:T(8,128)(2,1)S(1)} all-gather(bf16[12,1,16,128]{3,2,1,0:T(8,128)(2,1)S(1)} %get-tuple-element.260), channel_id=2, replica_groups=mesh['fx'=16,'fy'=16] {'fy'}, dimensions={2}, use_global_device_ids=true | all-gather | bytes 835584 | tf_op jit(solution)/shard_map/all_gather | solution.py:110
  130.8 0.9 broadcast_select_fusion.1
  131.7 20.0 %all-gather.1 = bf16[12,1,256,128]{3,2,1,0:T(8,128)(2,1)S(1)} all-gather(bf16[12,1,16,128]{3,2,1,0:T(8,128)(2,1)S(1)} %get-tuple-element.261), channel_id=3, replica_groups=mesh['fx'=16,'fy'=16] {'fy'}, dimensions={2}, use_global_device_ids=true | all-gather | bytes 835584 | tf_op jit(solution)/shard_map/all_gather | solution.py:111
  151.8 1.0 broadcast_select_fusion
  154.3 1.3 collective-permute-start.2
  155.6 3.5 collective-permute-start.3
  159.6 0.8 pad_maximum_fusion.2
  160.4 70.8 %all-reduce.12.cloned.1.call-done = (bf16[12,1,256,128]{3,2,1,0:T(8,128)(2,1)}, bf16[12,1,256,128]{3,2,0,1:T(8,128)(2,1)}) async-done(((bf16[12,1,256,128]{3,2,1,0:T(8,128)(2,1)}, bf16[12,1,256,128]{3,2,0,1:T(8,128)(2,1)}), (bf16[12,1,256,128]{3,2,1,0:T(8,128)(2,1)}, bf16[12,1,256,128]{3,2,0,1:T(8,128)(2,1)})) %all-reduce.12.cloned.1.call-update) | async-done | bytes 1572880 | tf_op jit(solution)/shard_map/psum | solution.py:9
  231.2 167.3 %all-reduce.14.cloned.1.call-done = (bf16[12,1,256,128]{3,2,1,0:T(8,128)(2,1)}, bf16[12,1,256,128]{3,2,1,0:T(8,128)(2,1)}) async-done(((bf16[12,1,256,128]{3,2,1,0:T(8,128)(2,1)}, bf16[12,1,256,128]{3,2,1,0:T(8,128)(2,1)}), (bf16[12,1,256,128]{3,2,1,0:T(8,128)(2,1)}, bf16[12,1,256,128]{3,2,1,0:T(8,128)(2,1)})) %all-reduce.14.cloned.1.call-update) | async-done | bytes 1572880 | tf_op jit(solution)/shard_map/psum | solution.py:9
  398.5 3.2 pad_maximum_fusion
  401.7 2.7 gather_fusion
  404.5 8.0 gather_fusion.2
  412.5 8.0 gather_fusion.1
  421.1 2.3 scatter.16
  423.6 2.4 scatter.19
  429.0 0.8 copy-done.3
  429.8 2.4 multiply_convert_fusion
  432.1 0.9 fusion.1
  433.0 0.9 fusion.2
  433.9 0.9 fusion.3
  434.7 0.9 fusion.4
  435.6 0.9 fusion.5
  436.5 0.9 fusion.6
  437.4 0.9 fusion.7
  438.2 0.9 fusion
  439.1 1.3 add_add_fusion
  440.9 12.1 %collective-permute-start.4 = (bf16[12,18,128]{2,1,0:T(8,128)(2,1)S(1)}, bf16[12,18,128]{2,1,0:T(8,128)(2,1)S(1)}, u32[]{:S(2)}, u32[]{:S(2)}) collective-permute-start(bf16[12,18,128]{2,1,0:T(8,128)(2,1)S(1)} %get-tuple-element.255), channel_id=1, source_target_pairs={{1,0},{2,1},{3,2},{4,3},{5,4},{6,5},{7,6},{8,7},{9,8},{10,9},{11,1... | collective-permute-start | bytes 165896 | tf_op jit(solution)/shard_map/ppermute | solution.py:32
  453.5 1.3 collective-permute-start.5
  455.0 2.4 scatter-add.54
  457.5 2.2 scatter-add.55
  459.8 1.3 collective-permute-start.6
  461.4 4.0 collective-permute-start.7
  465.4 1.4 collective-permute-done.7
  467.7 0.7 slice.926
  469.0 1.5 scatter-add.66
  470.5 1.4 scatter-add.70
  471.9 0.8 fusion.111
  472.8 1.5 scatter-add.69
  474.2 1.4 scatter-add.71
  475.7 0.9 fusion.45
  476.6 0.7 pad_maximum_fusion.4
  477.4 1.4 scatter-add.64
  478.8 0.8 fusion.107
  479.7 1.5 scatter-add.65
  481.2 0.6 pad_maximum_fusion.3
  481.9 117.3 %all-reduce.10.cloned.1.call-done = bf16[12,2,16,128]{3,2,0,1:T(8,128)(2,1)} async-done(((bf16[12,2,16,128]{3,2,0,1:T(8,128)(2,1)}), bf16[12,2,16,128]{3,2,0,1:T(8,128)(2,1)}) %all-reduce.10.cloned.1.call-update) | async-done | bytes 98320 | tf_op jit(solution)/shard_map/psum | solution.py:173
  599.3 153.2 %all-reduce.8.cloned.1.call-done = bf16[12,2,16,128]{3,2,0,1:T(8,128)(2,1)} async-done(((bf16[12,2,16,128]{3,2,0,1:T(8,128)(2,1)}), bf16[12,2,16,128]{3,2,0,1:T(8,128)(2,1)}) %all-reduce.8.cloned.1.call-update) | async-done | bytes 98320 | tf_op jit(solution)/shard_map/psum | solution.py:171
  752.9 1.3 slice.905
  754.3 64.2 %all-gather.9.cloned.1.call-done = bf16[12,2,256,128]{3,2,0,1:T(8,128)(2,1)} async-done(((bf16[12,2,16,128]{3,2,0,1:T(8,128)(2,1)}), bf16[12,2,256,128]{3,2,0,1:T(8,128)(2,1)}) %all-gather.9.cloned.1.call-update) | async-done | bytes 1572880 | tf_op jit(solution)/shard_map/all_gather | solution.py:174
  818.5 39.1 %all-gather.7.cloned.1.call-done = bf16[12,2,256,128]{3,2,0,1:T(8,128)(2,1)} async-done(((bf16[12,2,16,128]{3,2,0,1:T(8,128)(2,1)}), bf16[12,2,256,128]{3,2,0,1:T(8,128)(2,1)}) %all-gather.7.cloned.1.call-update) | async-done | bytes 1572880 | tf_op jit(solution)/shard_map/all_gather | solution.py:172
  857.6 2.2 pad_maximum_fusion.1
  859.7 2.0 copy.135
  861.7 7.9 gather_fusion.4
  869.7 8.0 gather_fusion.3
  877.9 2.0 scatter-add.76
  880.0 2.0 scatter-add.79
  881.9 1.0 convert_element_type.119
  (137 shorter events, 10.2 us)
Async XLA Ops:
  7.2 224.1 %all-reduce.12.cloned.1.call-start = ((), (), s32[]{:S(2)}) async-start(), calls=%async_computation.4 | async-start | bytes 3145728 | tf_op jit(solution)/shard_map/psum | solution.py:9
  91.7 1.4 copy-start.1
  92.7 305.8 %all-reduce.14.cloned.1.call-start = ((), (), s32[]{:S(2)}) async-start(), calls=%async_computation.5 | async-start | bytes 3145728 | tf_op jit(solution)/shard_map/psum | solution.py:9
  93.2 61.0 %collective-permute-start.1 = (bf16[12,1,16,128]{3,2,1,0:T(8,128)(2,1)S(1)}, bf16[12,1,16,128]{3,2,1,0:T(8,128)(2,1)S(1)}, u32[]{:S(2)}, u32[]{:S(2)}) collective-permute-start(bf16[12,1,16,128]{3,2,1,0:T(8,128)(2,1)S(1)} %get-tuple-element.260), channel_id=1, source_target_pairs={{16,0},{32,16},{48,32},{64,48},{80,64},{96,80},{112,96},{128,112},... | collective-permute-start | bytes 147464 | tf_op jit(solution)/shard_map/ppermute | solution.py:22
  94.5 59.5 %collective-permute-start = (bf16[12,1,16,128]{3,2,1,0:T(8,128)(2,1)S(1)}, bf16[12,1,16,128]{3,2,1,0:T(8,128)(2,1)S(1)}, u32[]{:S(2)}, u32[]{:S(2)}) collective-permute-start(bf16[12,1,16,128]{3,2,1,0:T(8,128)(2,1)S(1)} %get-tuple-element.261), channel_id=1, source_target_pairs={{0,16},{16,32},{32,48},{48,64},{64,80},{80,96},{96,112},{112,128},... | collective-permute-start | bytes 147464 | tf_op jit(solution)/shard_map/ppermute | solution.py:20
  151.8 1.1 copy-start.6
  151.8 1.2 copy-start.4
  151.8 1.2 copy-start.5
  152.7 446.5 %all-reduce.10.cloned.1.call-start = ((), (), s32[]{:S(2)}) async-start(), calls=%async_computation.2 | async-start | bytes 196608 | tf_op jit(solution)/shard_map/psum | solution.py:173
  154.3 5.2 collective-permute-start.2
  155.6 4.0 collective-permute-start.3
  420.5 5.5 copy-start.2
  428.6 1.1 copy-start.3
  428.6 1.1 copy-start.7
  440.9 13.9 %collective-permute-start.4 = (bf16[12,18,128]{2,1,0:T(8,128)(2,1)S(1)}, bf16[12,18,128]{2,1,0:T(8,128)(2,1)S(1)}, u32[]{:S(2)}, u32[]{:S(2)}) collective-permute-start(bf16[12,18,128]{2,1,0:T(8,128)(2,1)S(1)} %get-tuple-element.255), channel_id=1, source_target_pairs={{1,0},{2,1},{3,2},{4,3},{5,4},{6,5},{7,6},{8,7},{9,8},{10,9},{11,1... | collective-permute-start | bytes 165896 | tf_op jit(solution)/shard_map/ppermute | solution.py:32
  453.5 3.9 collective-permute-start.5
  459.8 5.6 collective-permute-start.6
  461.4 5.4 collective-permute-start.7
  477.3 275.2 %all-reduce.8.cloned.1.call-start = ((), (), s32[]{:S(2)}) async-start(), calls=%async_computation | async-start | bytes 196608 | tf_op jit(solution)/shard_map/psum | solution.py:171
  481.9 336.6 %all-gather.9.cloned.1.call-start = ((), (), s32[]{:S(2)}) async-start(), calls=%async_computation.3 | async-start | bytes 1671168 | tf_op jit(solution)/shard_map/all_gather | solution.py:174
  599.2 258.4 %all-gather.7.cloned.1.call-start = ((), (), s32[]{:S(2)}) async-start(), calls=%async_computation.1 | async-start | bytes 1671168 | tf_op jit(solution)/shard_map/all_gather | solution.py:172
  861.7 16.0 %copy-start = (f32[12,16,16,128]{3,2,1,0:T(8,128)S(1)}, f32[12,16,16,128]{3,2,1,0:T(8,128)}, u32[]{:S(2)}) copy-start(f32[12,16,16,128]{3,2,1,0:T(8,128)} %slice.905) | copy-start | bytes 4718596
Sparse Core Ops, SparseCore 0:
  92.8 138.3 all-reduce.11
  234.1 164.3 all-reduce.13
  477.4 121.7 all-reduce.9
  601.9 150.6 all-reduce.7
  754.8 63.6 all-gather.8
  820.1 37.4 all-gather.6
where the time goes:
time: 903 us; the launch traced here: 890 us
  waiting for transfers between devices  613 us (68%)
  blocking collectives  134 us (15%)
  local copies, waits for them, and re-layouts  67.6 us (7%)
  starting transfers between devices  29.3 us (3%)
  other arithmetic  16.5 us (2%)
  between operations  15.3 us (2%)
  matrix products  13.5 us (1%)
    psum x2, waiting for transfers between devices, spread_2(): return lax.psum(block, axis)  238 us
    psum x1, waiting for transfers between devices, shards(): lax.psum(row_cycles, 'fx').astype(jnp.float32).astype(jnp.bfloat16)  153 us
    psum x1, waiting for transfers between devices, shards(): lax.psum(col_cycles, 'fy').astype(jnp.float32).astype(jnp.bfloat16)  117 us
    all_gather x1, waiting for transfers between devices, shards(): col_whole = lax.all_gather(col_across, 'fx', axis=2, tiled=True)  64.2 us
    all_gather x1, blocking collectives, shards(): lax.all_gather(east_strip, 'fx', axis=1, tiled=True)  44.5 us
    all_gather x1, waiting for transfers between devices, shards(): row_whole = lax.all_gather(row_across, 'fy', axis=2, tiled=True)  39.1 us
    all_gather x1, blocking collectives, shards(): lax.all_gather(west_strip, 'fx', axis=1, tiled=True)  37.8 us
    gather x7, local copies, waits for them, and re-layouts, oriented(): return edge_lines[seam_face[:, :, None], seam_edge[:, :, None], turned]  34.6 us
  transfers between devices with their start and end apart: 14, of which 8 were waited for; matrix products, arithmetic and copies ran while one was open for 2% of the time, Pallas kernels for 0%

commit v1 on v0

v1 whole, which is shorter than its diff:
```python
import functools

import jax
import jax.numpy as jnp
from jax import lax
from jax.experimental import pallas as pl
from jax.experimental.pallas import tpu as pltpu
from jax.sharding import PartitionSpec as P

MESH = pl.DeviceIdType.MESH
F32 = jnp.float32
BF16 = jnp.bfloat16


def dot(a, b):
    return jnp.dot(a, b, preferred_element_type=F32)


def rows_iota(shape):
    return lax.broadcasted_iota(jnp.int32, shape, 0)


def cols_iota(shape):
    return lax.broadcasted_iota(jnp.int32, shape, 1)


def shifted_sum(taps, run):
    total, width = taps.shape[0], taps.shape[1] // 3
    place = rows_iota((total, width)) % run
    below = jnp.where(place == 0, 0.0, pltpu.roll(taps[:, :width], 1, 0))
    above = jnp.where(place == run - 1, 0.0, pltpu.roll(taps[:, 2 * width:], total - 1, 0))
    return taps[:, width:2 * width] + below + above


def silu_parts(value):
    sigma = 1.0 / (1.0 + jnp.exp(-value))
    return value * sigma, sigma * (1.0 + value * (1.0 - sigma))


def kernel(nx, ny, faces, side, width,
           face_tab, edge_tab, flip_tab, bias_ref, x_hbm, w_hbm, cot_hbm,
           act_out, grad_out,
           xp, cot, w9, acc, sp, act, grad,
           wf, wcol, vf, vcol, colcot, ring,
           src, corner_src, strip_in, corner_in, seam_a, seam_b, seam_c, seam_d, ends,
           near_send, near_recv, seam_send, seam_recv, ends_send, ends_recv, load_sem, store_sem):
    x = lax.axis_index("fx")
    y = lax.axis_index("fy")
    top, bottom, left, right = x == 0, x == nx - 1, y == 0, y == ny - 1
    row_rim = jnp.logical_or(top, bottom)
    col_rim = jnp.logical_or(left, right)
    seam = ((seam_a, seam_b), (seam_c, seam_d))
    cells = side * side
    strip = faces * side
    row_edge = x // (nx - 1)
    col_edge = 2 + y // (ny - 1)
    rims = ((row_rim, row_edge, y, ny), (col_rim, col_edge, x, nx))

    near = []
    for dx, dy, slot in ((-1, 0, 0), (1, 0, 1), (0, -1, 2), (0, 1, 3), (-1, -1, 4), (-1, 1, 5), (1, -1, 6), (1, 1, 7)):
        tx, ty = x + dx, y + dy
        inside = None
        for ok in ([tx >= 0] if dx < 0 else [tx < nx] if dx > 0 else []) + ([ty >= 0] if dy < 0 else [ty < ny] if dy > 0 else []):
            inside = ok if inside is None else jnp.logical_and(inside, ok)
        back = slot ^ 1 if slot < 4 else 4 + (3 - (slot - 4))
        near.append((tx, ty, inside, slot, back))

    def seam_target(kind, count, place, step):
        half, turn = step // 2, step % 2
        spot = place + turn * (count - 1 - 2 * place)
        if kind == 0:
            tx, ty = half * (nx - 1), spot
        else:
            tx, ty = spot, half * (ny - 1)
        mine = jnp.logical_and(tx == x, ty == y)
        return turn, tx, ty, mine

    def ends_target(kind, count, place, step):
        half, end, turn = step // 4, (step // 2) % 2, step % 2
        cell = (end + turn + 1) % 2
        spot = place + 1 - 2 * end + turn * (count - 1 - 2 * place)
        valid = jnp.logical_and(spot >= 0, spot < count)
        if kind == 0:
            tx, ty = half * (nx - 1), spot
        else:
            tx, ty = spot, half * (ny - 1)
        mine = jnp.logical_and(tx == x, ty == y)
        return end, turn, cell, tx, ty, valid, mine

    def near_copy(trip, item):
        tx, ty, inside, slot, back = item
        if slot < 4:
            source, target = src.at[trip, 0, slot], strip_in.at[trip, back]
        else:
            source, target = corner_src.at[trip, slot - 4], corner_in.at[trip, back - 4]
        return pltpu.make_async_remote_copy(
            src_ref=source, dst_ref=target, send_sem=near_send.at[trip, slot], recv_sem=near_recv.at[trip, back],
            device_id=(tx, ty), device_id_type=MESH)

    def near_arrival(trip, slot):
        here = strip_in.at[trip, slot] if slot < 4 else corner_in.at[trip, slot - 4]
        return pltpu.make_async_copy(here, here, near_recv.at[trip, slot])

    def seam_copy(away, trip, rim, edge, kind, step, turn, tx, ty):
        source = src.at[trip, turn, edge]
        target = seam[trip][kind].at[turn, edge]
        if not away:
            return pltpu.make_async_copy(source, target, seam_recv.at[trip, kind])
        return pltpu.make_async_remote_copy(
            src_ref=source, dst_ref=target, send_sem=seam_send.at[trip, rim, kind, step],
            recv_sem=seam_recv.at[trip, kind], device_id=(tx, ty), device_id_type=MESH)

    def ends_copy(away, trip, rim, edge, kind, step, end, turn, cell, tx, ty):
        which = 2 * edge + cell if rim == 0 else edge - 2 + 2 * cell
        source = corner_src.at[trip, which]
        target = ends.at[trip, kind, end, turn, edge]
        if not away:
            return pltpu.make_async_copy(source, target, ends_recv.at[trip, kind, end])
        return pltpu.make_async_remote_copy(
            src_ref=source, dst_ref=target, send_sem=ends_send.at[trip, rim, kind, step],
            recv_sem=ends_recv.at[trip, kind, end], device_id=(tx, ty), device_id_type=MESH)

    def each_far(act_on):
        for rim, (active, edge, place, count) in enumerate(rims):
            @pl.when(active)
            def _(rim=rim, edge=edge, place=place, count=count):
                for kind in range(2):
                    def seam_step(step, carry, kind=kind):
                        turn, tx, ty, mine = seam_target(kind, count, place, step)
                        act_on("seam", rim, edge, kind, step, (turn, tx, ty), None, mine)
                        return carry
                    lax.fori_loop(0, 4, seam_step, 0)
                for kind in range(2):
                    def ends_step(step, carry, kind=kind):
                        end, turn, cell, tx, ty, valid, mine = ends_target(kind, count, place, step)
                        act_on("ends", rim, edge, kind, step, (end, turn, cell, tx, ty), valid, mine)
                        return carry
                    lax.fori_loop(0, 8, ends_step, 0)

    def send_all(trip):
        for item in near:
            @pl.when(item[2])
            def _(item=item):
                near_copy(trip, item).start()

        def begin(sort, rim, edge, kind, step, rest, valid, mine):
            copy = seam_copy if sort == "seam" else ends_copy
            far_on = jnp.logical_not(mine)
            if valid is not None:
                far_on = jnp.logical_and(far_on, valid)
                mine = jnp.logical_and(mine, valid)

            @pl.when(far_on)
            def _():
                copy(True, trip, rim, edge, kind, step, *rest).start()

            @pl.when(mine)
            def _():
                copy(False, trip, rim, edge, kind, step, *rest).start()

        each_far(begin)

    def wait_sent(trip):
        for item in near:
            @pl.when(item[2])
            def _(item=item):
                near_copy(trip, item).wait_send()

        def finish(sort, rim, edge, kind, step, rest, valid, mine):
            copy = seam_copy if sort == "seam" else ends_copy
            far_on = jnp.logical_not(mine)
            if valid is not None:
                far_on = jnp.logical_and(far_on, valid)

            @pl.when(far_on)
            def _():
                copy(True, trip, rim, edge, kind, step, *rest).wait_send()

        each_far(finish)

    first_last = jnp.where(
        jnp.logical_and(
            cols_iota((32, strip)) == (rows_iota((32, strip)) % 16) * side + (rows_iota((32, strip)) // 16) * (side - 1),
            rows_iota((32, strip)) % 16 < faces),
        1.0, 0.0).astype(BF16)

    def turned(trip):
        def turn_one(edge):
            back = rows_iota((strip, strip)) - 2 * (rows_iota((strip, strip)) % side) + (side - 1)
            turner = jnp.where(back == cols_iota((strip, strip)), 1.0, 0.0).astype(BF16)
            line = src[trip, 0, edge].reshape(strip, width)
            src[trip, 1, edge] = dot(turner, line).astype(BF16).reshape(faces, side, width)

        @pl.when(row_rim)
        def _():
            turn_one(row_edge)

        @pl.when(col_rim)
        def _():
            turn_one(col_edge)

    def arrivals(trip):
        for item in near:
            @pl.when(item[2])
            def _(item=item):
                near_arrival(trip, item[3]).wait()
        for rim, (active, edge, place, count) in enumerate(rims):
            @pl.when(active)
            def _(rim=rim, edge=edge, place=place, count=count):
                whole = seam[trip][rim]
                pltpu.make_async_copy(whole, whole, seam_recv.at[trip, rim]).wait()

                def pick(f, carry):
                    strip_in[trip, edge, f] = seam[trip][rim][flip_tab[f, edge], edge_tab[f, edge], face_tab[f, edge]]
                    return carry
                lax.fori_loop(0, faces, pick, 0)

                chosen = jnp.zeros((16, 128), F32)
                for f in range(faces):
                    code = (flip_tab[f, edge] * 4 + edge_tab[f, edge]) * 16 + face_tab[f, edge]
                    hit = jnp.logical_and(rows_iota((16, 128)) == f, cols_iota((16, 128)) == code)
                    chosen = jnp.where(hit, 1.0, chosen)
                chosen = chosen.astype(BF16)
                for end in range(2):
                    @pl.when(place > 0 if end == 0 else place < count - 1)
                    def _(end=end):
                        part = ends.at[trip, rim, end]
                        pltpu.make_async_copy(part, part, ends_recv.at[trip, rim, end]).wait()
                        value = dot(chosen, ends[trip, rim, end].reshape(128, width)).astype(BF16)
                        if rim == 0:
                            corner_in[trip, 2 * edge + end] = value
                        else:
                            corner_in[trip, edge - 2 + 2 * end] = value

        @pl.when(jnp.logical_and(row_rim, col_rim))
        def _():
            which = 2 * row_edge + col_edge - 2
            if trip == 0:
                ends_a = dot(first_last, strip_in[0, row_edge].reshape(strip, width))
                ends_b = dot(first_last, strip_in[0, col_edge].reshape(strip, width))
                at_a = jnp.where(left, ends_a[:16], ends_a[16:])
                at_b = jnp.where(top, ends_b[:16], ends_b[16:])
                corner_in[0, which] = (0.5 * (at_a + at_b)).astype(BF16)
            else:
                corner_in[1, which] = jnp.zeros((16, width), BF16)

    load_x = pltpu.make_async_copy(x_hbm, xp.at[:, 1:side + 1], load_sem.at[0])
    load_w = pltpu.make_async_copy(w_hbm, w9, load_sem.at[1])
    load_c = pltpu.make_async_copy(cot_hbm, cot, load_sem.at[2])
    load_x.start()
    load_w.start()
    load_c.start()

    barrier = pltpu.get_barrier_semaphore()
    due = jnp.int32(0)
    for tx, ty, inside, slot, back in near:
        @pl.when(inside)
        def _(tx=tx, ty=ty):
            pl.semaphore_signal(barrier, inc=1, device_id=(tx, ty), device_id_type=MESH)
        due = due + inside.astype(jnp.int32)
    for rim, (active, edge, place, count) in enumerate(rims):
        def signal_if(on, tx, ty):
            @pl.when(on)
            def _():
                pl.semaphore_signal(barrier, inc=1, device_id=(tx, ty), device_id_type=MESH)
        for kind in range(2):
            def seam_step(step, total, kind=kind, active=active, place=place, count=count):
                turn, tx, ty, mine = seam_target(kind, count, place, step)
                on = jnp.logical_and(active, jnp.logical_not(mine))
                signal_if(on, tx, ty)
                return total + on.astype(jnp.int32)
            due = lax.fori_loop(0, 4, seam_step, due)

            def ends_step(step, total, kind=kind, active=active, place=place, count=count):
                end, turn, cell, tx, ty, valid, mine = ends_target(kind, count, place, step)
                on = jnp.logical_and(jnp.logical_and(active, valid), jnp.logical_not(mine))
                signal_if(on, tx, ty)
                return total + on.astype(jnp.int32)
            due = lax.fori_loop(0, 8, ends_step, due)

    zero_rows = jnp.zeros((faces, side, width), BF16)
    xp[:, 0] = zero_rows
    xp[:, side + 1] = zero_rows
    sp[:, 0] = zero_rows
    sp[:, side + 1] = zero_rows
    load_x.wait()
    src[0, 0, 0] = xp[:, 1]
    src[0, 0, 1] = xp[:, side]
    column_pick = jnp.where(
        cols_iota((2 * side, cells)) == (rows_iota((2 * side, cells)) % side) * side
        + (rows_iota((2 * side, cells)) // side) * (side - 1), 1.0, 0.0).astype(BF16)
    for f in range(faces):
        both = dot(column_pick, xp[f, 1:side + 1].reshape(cells, width)).astype(BF16)
        src[0, 0, 2, f] = both[:side]
        src[0, 0, 3, f] = both[side:]
    for half in range(2):
        picked = dot(first_last, src[0, 0, half].reshape(strip, width)).astype(BF16)
        corner_src[0, 2 * half] = picked[:16]
        corner_src[0, 2 * half + 1] = picked[16:]
    turned(0)
    pl.semaphore_wait(barrier, due)
    send_all(0)

    load_w.wait()
    for a in range(3):
        for b in range(3):
            tap = w9[a, b]
            back = tap.astype(F32).T.astype(BF16)
            wf[a * width:(a + 1) * width, b * width:(b + 1) * width] = tap
            vf[(2 - a) * width:(3 - a) * width, (2 - b) * width:(3 - b) * width] = back
            if b != 1:
                wcol[b // 2, :, a * width:(a + 1) * width] = tap
                vcol[b // 2, :, (2 - a) * width:(3 - a) * width] = back
    load_c.wait()
    for f in range(faces):
        both = dot(column_pick, cot[f].reshape(cells, width))
        colcot[0, f * side:(f + 1) * side] = both[:side]
        colcot[1, f * side:(f + 1) * side] = both[side:]

    def conv(source, f, weights):
        stacked = jnp.concatenate(
            [source[f, a:a + side].reshape(cells, width) for a in range(3)], axis=1)
        return shifted_sum(dot(stacked, weights), side)

    def forward_face(f, carry):
        acc[pl.ds(pl.multiple_of(f * cells, cells), cells)] = conv(xp, f, wf[...]) + bias_ref[...]
        return carry
    lax.fori_loop(0, faces, forward_face, 0)

    def add_rim(strips, corners):
        for half in range(2):
            line = strips[half]
            for f in range(faces):
                at = f * cells + half * (cells - side)
                acc[at:at + side] += line[f * side:(f + 1) * side]
        for half in range(2):
            at = pl.ds(half * (side - 1), strip, stride=side)
            acc[at] = acc[at] + strips[2 + half]
        for which in range(4):
            at = pl.ds((which // 2) * (cells - side) + (which % 2) * (side - 1), faces, stride=cells)
            acc[at] = acc[at] + corners[which]

    arrivals(0)
    strips = []
    for edge in range(4):
        line = strip_in[0, edge].reshape(strip, width)
        weights = wf[2 * edge * width:(2 * edge + 1) * width] if edge < 2 else wcol[edge - 2]
        strips.append(shifted_sum(dot(line, weights), side))
    corners = [dot(corner_in[0, 2 * a + b], w9[2 * a, 2 * b])[:faces] for a in range(2) for b in range(2)]
    add_rim(strips, corners)

    rim_slopes = []
    for half in range(2):
        at = half * (cells - side)
        line = jnp.concatenate([acc[f * cells + at:f * cells + at + side] for f in range(faces)], axis=0)
        rim_slopes.append((cot[:, half * (side - 1)].reshape(strip, width).astype(F32) * silu_parts(line)[1]).astype(BF16))
    for half in range(2):
        line = acc[pl.ds(half * (side - 1), strip, stride=side)]
        rim_slopes.append((colcot[half] * silu_parts(line)[1]).astype(BF16))
    for edge in range(4):
        weights = vf[2 * (1 - edge) * width:(2 * (1 - edge) + 1) * width] if edge < 2 else vcol[edge - 2]
        ring[edge] = shifted_sum(dot(rim_slopes[edge], weights), side)
    for a in range(2):
        picked = dot(first_last, rim_slopes[a]).astype(BF16)
        for b in range(2):
            beyond = dot(picked[16 * b:16 * b + 16], vf[2 * (1 - a) * width:(2 * (1 - a) + 1) * width,
                                                        2 * (1 - b) * width:(2 * (1 - b) + 1) * width])
            corner_src[1, 2 * a + b] = beyond.astype(BF16)

            @pl.when(jnp.logical_and(bottom if a else top, right if b else left))
            def _(a=a, b=b, beyond=beyond):
                along_row = pl.ds(b * (side - 1), faces, stride=side)
                along_col = pl.ds(a * (side - 1), faces, stride=side)
                ring[a, along_row] = ring[a, along_row] + 0.5 * beyond[:faces]
                ring[2 + b, along_col] = ring[2 + b, along_col] + 0.5 * beyond[:faces]
    for edge in range(4):
        src[1, 0, edge] = ring[edge].astype(BF16).reshape(faces, side, width)
    turned(1)
    send_all(1)

    def adjoint_face(f, carry):
        at = pl.ds(pl.multiple_of(f * cells, cells), cells)
        value, slope = silu_parts(acc[at])
        act[f] = value.astype(BF16).reshape(side, side, width)
        slope = cot[f].reshape(cells, width).astype(F32) * slope
        sp[f, 1:side + 1] = slope.astype(BF16).reshape(side, side, width)
        acc[at] = conv(sp, f, vf[...])
        return carry
    lax.fori_loop(0, faces, adjoint_face, 0)
    store_act = pltpu.make_async_copy(act, act_out, store_sem.at[0])
    store_act.start()

    arrivals(1)
    add_rim([strip_in[1, edge].reshape(strip, width).astype(F32) for edge in range(4)],
            [corner_in[1, which].astype(F32)[:faces] for which in range(4)])

    def finish_face(f, carry):
        at = pl.ds(pl.multiple_of(f * cells, cells), cells)
        grad[f] = acc[at].astype(BF16).reshape(side, side, width)
        return carry
    lax.fori_loop(0, faces, finish_face, 0)
    store_grad = pltpu.make_async_copy(grad, grad_out, store_sem.at[1])
    store_grad.start()
    wait_sent(0)
    wait_sent(1)
    store_act.wait()
    store_grad.wait()


def shards(features, weight, out_bias, cotangent, seam_face, seam_edge, seam_flip):
    faces, side, _, width = features.shape
    nx, ny = lax.axis_size("fx"), lax.axis_size("fy")
    patch = (faces, side, side, width)
    padded = (faces, side + 2, side, width)
    strip = faces * side
    dma = pltpu.SemaphoreType.DMA
    anywhere = pl.BlockSpec(memory_space=pl.ANY)
    table = pl.BlockSpec(memory_space=pltpu.SMEM)
    return pl.pallas_call(
        functools.partial(kernel, nx, ny, faces, side, width),
        out_shape=(jax.ShapeDtypeStruct(patch, BF16), jax.ShapeDtypeStruct(patch, BF16)),
        in_specs=[table, table, table, pl.BlockSpec(memory_space=pltpu.VMEM), anywhere, anywhere, anywhere],
        out_specs=(anywhere, anywhere),
        scratch_shapes=[
            pltpu.VMEM(padded, BF16),
            pltpu.VMEM(patch, BF16),
            pltpu.VMEM((3, 3, width, width), BF16),
            pltpu.VMEM((faces * side * side, width), F32),
            pltpu.VMEM(padded, BF16),
            pltpu.VMEM(patch, BF16),
            pltpu.VMEM(patch, BF16),
            pltpu.VMEM((3 * width, 3 * width), BF16),
            pltpu.VMEM((2, width, 3 * width), BF16),
            pltpu.VMEM((3 * width, 3 * width), BF16),
            pltpu.VMEM((2, width, 3 * width), BF16),
            pltpu.VMEM((2, strip, width), F32),
            pltpu.VMEM((4, strip, width), F32),
            pltpu.VMEM((2, 2, 4, faces, side, width), BF16),
            pltpu.VMEM((2, 4, 16, width), BF16),
            pltpu.VMEM((2, 4, faces, side, width), BF16),
            pltpu.VMEM((2, 4, 16, width), BF16),
            *[pltpu.VMEM((2, 4, faces, side, width), BF16)] * 4,
            pltpu.VMEM((2, 2, 2, 2, 4, 16, width), BF16),
            dma((2, 8)),
            dma((2, 8)),
            dma((2, 2, 2, 4)),
            dma((2, 2)),
            dma((2, 2, 2, 8)),
            dma((2, 2, 2)),
            dma((3,)),
            dma((2,)),
        ],
        compiler_params=pltpu.CompilerParams(
            collective_id=0, has_side_effects=True, vmem_limit_bytes=40 * 1024 * 1024),
    )(seam_face, seam_edge, seam_flip, out_bias.reshape(1, width), features, weight, cotangent)


def solution(mesh):
    in_specs = (P(None, "fx", "fy", None), P(), P(), P(None, "fx", "fy", None), P(), P(), P())
    out_specs = (P(None, "fx", "fy", None), P(None, "fx", "fy", None))
    return jax.shard_map(shards, mesh=mesh, in_specs=in_specs, out_specs=out_specs, check_vma=False)
```

time: 903 us -> 59.2 us (0.07); the launches traced: 890 us -> 58.2 us
  waiting for transfers between devices: 613 us -> 0 us
  blocking collectives: 134 us -> 0 us
  local copies, waits for them, and re-layouts: 67.6 us -> 7.1 us
  Pallas kernels: 0 us -> 50.4 us
  starting transfers between devices: 29.3 us -> 0 us
  other arithmetic: 16.5 us -> 0 us
  between operations: 15.3 us -> 0.65 us
  matrix products: 13.5 us -> 0 us
    psum x4 -> x0, waiting for transfers between devices: 509 us -> none  [the longest x2 238 us: spread_2(): return lax.psum(block, axis)]
    all_gather x4 -> x0, blocking collectives: 134 us -> none  [the longest x1 44.5 us: shards(): lax.all_gather(east_strip, 'fx', axis=1, tiled=True)]
    all_gather x2 -> x0, waiting for transfers between devices: 103 us -> none  [the longest x1 64.2 us: shards(): col_whole = lax.all_gather(col_across, 'fx', axis=2, tiled=True)]
    pallas_call x0 -> x1, Pallas kernels: none -> 50.4 us  [shards(): pl.pallas_call(functools.partial(kernel, nx, ny, faces, side, width), out...]
    gather x7 -> x0, local copies, waits for them, and re-layouts: 34.6 us -> none  [oriented(): return edge_lines[seam_face[:, :, None], seam_edge[:, :, None], turned]]
    ppermute x8 -> x0, starting transfers between devices: 29.1 us -> none  [the longest x4 18.7 us: passed_along(): lax.ppermute(value, axis, [(source, source + steps) for source in range(i...]
    scatter-add x14 -> x0, local copies, waits for them, and re-layouts: 17.6 us -> none  [the longest x3 4.87 us: shards(): spread = spread.at[:, :, -2].add(from_right).at[:, :, 1].add(from_left)]
    dot_general x18 -> x0, matrix products: 13.5 us -> none  [tap_sum(): jnp.einsum(einsum_form, window, weight[tap_row, tap_col], preferred_eleme...]
  transfers between devices with their start and end apart: 14 -> 0, of which waited for: 8 -> 0; matrix products, arithmetic and copies ran while one was open for 2% -> 0% of each run, Pallas kernels for 0% -> 0%
where the time goes in v1:
time: 59.2 us; the launch traced here: 58.2 us
  Pallas kernels  50.4 us (85%)
  local copies, waits for them, and re-layouts  7.1 us (12%)
  between operations  0.65 us (1%)
    pallas_call x1, Pallas kernels, shards(): pl.pallas_call(functools.partial(kernel, nx, ny, faces, side, width), out...  50.4 us
    unnamed x17, local copies, waits for them, and re-layouts  7.1 us

profile of v1, /device:TPU:57, one launch (start us, length us, event | category | flops | bytes accessed | tf_op | source)
XLA Modules:
  0.0 58.2 jit_solution(14011953882617137112)
XLA Ops:
  0.6 0.0 copy-start.4
  0.6 0.8 %copy.9.face_tab = s32[12,4]{1,0:T(8,128)S(1)} copy(s32[12,4]{0,1:T(4,128)} %param.11) | data formatting | bytes 384 | tf_op args[4]
  1.4 0.0 copy-done.4
  1.4 0.0 copy-start.5
  1.4 0.1 copy.10.edge_tab
  1.5 0.6 %copy-done.5 = s32[12,4]{0,1:T(4,128)S(1)} copy-done((s32[12,4]{0,1:T(4,128)S(1)}, s32[12,4]{0,1:T(4,128)}, u32[]{:S(2)}) %copy-start.5) | copy-done | bytes 216
  2.1 0.0 copy-start.3
  2.1 0.1 copy.11.flip_tab
  2.2 0.6 copy-done.3
  2.8 0.0 copy-start
  2.8 1.1 %copy-done = bf16[12,16,16,128]{3,2,1,0:T(8,128)(2,1)S(1)} copy-done((bf16[12,16,16,128]{3,2,1,0:T(8,128)(2,1)S(1)}, bf16[12,16,16,128]{3,2,1,0:T(8,128)(2,1)}, u32[]{:S(2)}) %copy-start) | copy-done | bytes 786456
  3.9 0.0 copy-start.1
  3.9 1.1 %copy-done.1 = bf16[12,16,16,128]{3,2,1,0:T(8,128)(2,1)S(1)} copy-done((bf16[12,16,16,128]{3,2,1,0:T(8,128)(2,1)S(1)}, bf16[12,16,16,128]{3,2,1,0:T(8,128)(2,1)}, u32[]{:S(2)}) %copy-start.1) | copy-done | bytes 786456
  5.0 0.0 copy-start.2
  5.0 1.0 %copy-done.2 = bf16[3,3,128,128]{3,2,1,0:T(8,128)(2,1)S(1)} copy-done((bf16[3,3,128,128]{3,2,1,0:T(8,128)(2,1)S(1)}, bf16[3,3,128,128]{3,2,1,0:T(8,128)(2,1)}, u32[]{:S(2)}) %copy-start.2) | copy-done | bytes 294936
  6.0 50.4 %shard_map.86 = (bf16[12,16,16,128]{3,2,1,0:T(8,128)(2,1)S(1)}, bf16[12,16,16,128]{3,2,1,0:T(8,128)(2,1)S(1)}) custom-call(s32[12,4]{1,0:T(8,128)S(1)} %copy.9.face_tab, s32[12,4]{1,0:T(8,128)S(1)} %copy.10.edge_tab, s32[12,4]{1,0:T(8,128)S(1)} %copy.11.flip_tab, f32[1,128]{1,0:T(1,128)S(1)} %bitcast.1, bf16[12,16,16,128]{3,2,1,0:T(8,128)(2,1)S(1)} %copy-done, ...), custom_call_target="tpu_custom_call" | custom-call | tf_op jit(solution)/shard_map/pallas_call | solution.py:419
  56.4 0.9 %copy.14 = bf16[12,16,16,128]{3,2,1,0:T(8,128)(2,1)} copy(bf16[12,16,16,128]{3,2,1,0:T(8,128)(2,1)S(1)} %get-tuple-element.4) | data formatting | bytes 1572864
  57.3 0.9 %copy.15 = bf16[12,16,16,128]{3,2,1,0:T(8,128)(2,1)} copy(bf16[12,16,16,128]{3,2,1,0:T(8,128)(2,1)S(1)} %get-tuple-element.5) | data formatting | bytes 1572864
Async XLA Ops:
  0.6 0.8 %copy-start.4 = (s32[12,4]{0,1:T(4,128)S(1)}, s32[12,4]{0,1:T(4,128)}, u32[]{:S(2)}) copy-start(s32[12,4]{0,1:T(4,128)} %param.12) | copy-start | bytes 580
  1.4 0.7 %copy-start.5 = (s32[12,4]{0,1:T(4,128)S(1)}, s32[12,4]{0,1:T(4,128)}, u32[]{:S(2)}) copy-start(s32[12,4]{0,1:T(4,128)} %param.13) | copy-start | bytes 580
  2.1 0.7 %copy-start.3 = (f32[128]{0:T(128)S(1)}, f32[128]{0:T(128)}, u32[]{:S(2)}) copy-start(f32[128]{0:T(128)} %param.9) | copy-start | bytes 1540
  2.8 1.1 %copy-start = (bf16[12,16,16,128]{3,2,1,0:T(8,128)(2,1)S(1)}, bf16[12,16,16,128]{3,2,1,0:T(8,128)(2,1)}, u32[]{:S(2)}) copy-start(bf16[12,16,16,128]{3,2,1,0:T(8,128)(2,1)} %x_hbm.1) | copy-start | bytes 2359300
  3.9 1.1 %copy-start.1 = (bf16[12,16,16,128]{3,2,1,0:T(8,128)(2,1)S(1)}, bf16[12,16,16,128]{3,2,1,0:T(8,128)(2,1)}, u32[]{:S(2)}) copy-start(bf16[12,16,16,128]{3,2,1,0:T(8,128)(2,1)} %cot_hbm.1) | copy-start | bytes 2359300
  5.0 1.0 %copy-start.2 = (bf16[3,3,128,128]{3,2,1,0:T(8,128)(2,1)S(1)}, bf16[3,3,128,128]{3,2,1,0:T(8,128)(2,1)}, u32[]{:S(2)}) copy-start(bf16[3,3,128,128]{3,2,1,0:T(8,128)(2,1)} %w_hbm.1) | copy-start | bytes 884740

commit v2 on v1

v2 whole, which is shorter than its diff:
```python
import functools

import jax
import jax.numpy as jnp
from jax import lax
from jax.experimental import pallas as pl
from jax.experimental.pallas import tpu as pltpu
from jax.sharding import PartitionSpec as P

MESH = pl.DeviceIdType.MESH
F32 = jnp.float32
BF16 = jnp.bfloat16


def dot(a, b):
    return jnp.dot(a, b, preferred_element_type=F32)


def rows_iota(shape):
    return lax.broadcasted_iota(jnp.int32, shape, 0)


def cols_iota(shape):
    return lax.broadcasted_iota(jnp.int32, shape, 1)


def shifted_sum(taps, run):
    total, width = taps.shape[0], taps.shape[1] // 3
    place = rows_iota((total, width)) % run
    below = jnp.where(place == 0, 0.0, pltpu.roll(taps[:, :width], 1, 0))
    above = jnp.where(place == run - 1, 0.0, pltpu.roll(taps[:, 2 * width:], total - 1, 0))
    return taps[:, width:2 * width] + below + above


def silu_parts(value):
    sigma = 1.0 / (1.0 + jnp.exp(-value))
    return value * sigma, sigma * (1.0 + value * (1.0 - sigma))


def kernel(nx, ny, faces, side, width,
           face_hbm, edge_hbm, flip_hbm, bias_hbm, x_hbm, w_hbm, cot_hbm,
           act, grad,
           face_tab, edge_tab, flip_tab, bias_ref, xp, cot, w9, acc, sp,
           wf, wcol, vf, vcol, colcot, ring, turner, chooser,
           src, corner_src, strip_in, corner_in, seam_first, seam_second, end_src,
           near_send, near_recv, seam_send, seam_recv, ends_send, load_sem):
    x = lax.axis_index("fx")
    y = lax.axis_index("fy")
    top, bottom, left, right = x == 0, x == nx - 1, y == 0, y == ny - 1
    row_rim = jnp.logical_or(top, bottom)
    col_rim = jnp.logical_or(left, right)
    rim = jnp.logical_or(row_rim, col_rim)
    corner = jnp.logical_and(row_rim, col_rim)
    seam = (seam_first, seam_second)
    cells = side * side
    strip = faces * side
    row_edge = x // (nx - 1)
    col_edge = 2 + y // (ny - 1)
    rims = ((row_rim, row_edge, y, ny, (y // (ny // 2)) * 4 + row_edge),
            (col_rim, col_edge, x, nx, (x // (nx // 2)) * 4 + col_edge))

    near = []
    for dx, dy, slot in ((-1, 0, 0), (1, 0, 1), (0, -1, 2), (0, 1, 3), (-1, -1, 4), (-1, 1, 5), (1, -1, 6), (1, 1, 7)):
        tx, ty = x + dx, y + dy
        inside = None
        for ok in ([tx >= 0] if dx < 0 else [tx < nx] if dx > 0 else []) + ([ty >= 0] if dy < 0 else [ty < ny] if dy > 0 else []):
            inside = ok if inside is None else jnp.logical_and(inside, ok)
        back = slot ^ 1 if slot < 4 else 4 + (3 - (slot - 4))
        near.append((tx, ty, inside, slot, back))

    def partners(which):
        active, edge, place, count, slot = rims[which]
        for kind in range(2):
            for half in range(2):
                for turn in range(2):
                    spot = count - 1 - place if turn else place
                    tx, ty = (half * (nx - 1), spot) if kind == 0 else (spot, half * (ny - 1))
                    other = jnp.logical_not(jnp.logical_and(tx == x, ty == y))
                    on = jnp.logical_and(active, other)
                    if kind == 1:
                        on = jnp.logical_and(on, jnp.logical_not(corner))
                    yield kind * 4 + half * 2 + turn, tx, ty, on

    def near_copy(trip, item):
        tx, ty, inside, slot, back = item
        if slot < 4:
            source, target = src.at[trip, slot], strip_in.at[trip, back]
        else:
            source, target = corner_src.at[trip, slot - 4], corner_in.at[trip, back - 4]
        return pltpu.make_async_remote_copy(
            src_ref=source, dst_ref=target, send_sem=near_send.at[trip, slot], recv_sem=near_recv.at[trip, back],
            device_id=(tx, ty), device_id_type=MESH)

    def near_arrival(trip, slot):
        here = strip_in.at[trip, slot] if slot < 4 else corner_in.at[trip, slot - 4]
        return pltpu.make_async_copy(here, here, near_recv.at[trip, slot])

    def seam_copy(trip, which, step, tx, ty):
        slot = rims[which][4]
        line = seam[trip].at[slot, 0:faces] if trip == 0 else seam[trip].at[slot]
        return pltpu.make_async_remote_copy(
            src_ref=line, dst_ref=line, send_sem=seam_send.at[trip, which, step],
            recv_sem=seam_recv.at[trip], device_id=(tx, ty), device_id_type=MESH)

    def end_copy(trip, which, end):
        active, edge, place, count, slot = rims[which]
        spot = place + 2 * end - 1
        if which == 0:
            tx, ty, back = x, spot, 2 * edge + 1 - end
        else:
            tx, ty, back = spot, y, edge - 2 + 2 * (1 - end)
        return pltpu.make_async_remote_copy(
            src_ref=end_src.at[trip, which, end], dst_ref=corner_in.at[trip, back],
            send_sem=ends_send.at[trip, which, end], recv_sem=near_recv.at[trip, 4 + back],
            device_id=(tx, ty), device_id_type=MESH)

    def send_all(trip):
        for which in range(2):
            for step, tx, ty, on in partners(which):
                @pl.when(on)
                def _(which=which, step=step, tx=tx, ty=ty):
                    seam_copy(trip, which, step, tx, ty).start()
        for item in near:
            @pl.when(item[2])
            def _(item=item):
                near_copy(trip, item).start()

    def wait_sent(trip):
        for which in range(2):
            for step, tx, ty, on in partners(which):
                @pl.when(on)
                def _(which=which, step=step, tx=tx, ty=ty):
                    seam_copy(trip, which, step, tx, ty).wait_send()
            active, edge, place, count, slot = rims[which]
            for end in range(2):
                @pl.when(jnp.logical_and(active, place < count - 1 if end else place > 0))
                def _(which=which, end=end):
                    end_copy(trip, which, end).wait_send()
        for item in near:
            @pl.when(item[2])
            def _(item=item):
                near_copy(trip, item).wait_send()

    first_last = jnp.where(
        jnp.logical_and(
            cols_iota((32, strip)) == (rows_iota((32, strip)) % 16) * side + (rows_iota((32, strip)) // 16) * (side - 1),
            rows_iota((32, strip)) % 16 < faces),
        1.0, 0.0).astype(BF16)

    def own_lines(trip):
        for which in range(2):
            active, edge, place, count, slot = rims[which]

            @pl.when(active)
            def _(which=which, edge=edge, slot=slot):
                seam[trip][slot, 0:faces] = src[trip, edge]
                if trip == 1:
                    for end in range(2):
                        at = 2 * edge + end if which == 0 else edge - 2 + 2 * end
                        seam[trip][slot, faces + end] = corner_src[trip, at]

    def prepare_choice():
        for which in range(2):
            active, edge, place, count, slot = rims[which]

            @pl.when(active)
            def _(which=which, edge=edge, place=place, count=count):
                row, col = rows_iota((strip, strip)), cols_iota((strip, strip))
                mirrored = row - 2 * (row % side) + (side - 1)
                end_row, end_col = rows_iota((16, 256)), cols_iota((16, 256))
                wanted = row
                chosen = [jnp.zeros((16, 256), F32)] * 2
                for f in range(faces):
                    flip = flip_tab[edge, f]
                    flipped = jnp.logical_and(row // side == f, jnp.full((strip, strip), flip, jnp.int32) == 1)
                    wanted = jnp.where(flipped, mirrored, wanted)
                    part = place // (count // 2)
                    part = part + flip * (1 - 2 * part)
                    for end in range(2):
                        code = ((part * 4 + edge_tab[edge, f]) * 2 + end + flip * (1 - 2 * end)) * 16 + face_tab[edge, f]
                        hit = jnp.logical_and(end_row == f, end_col == code)
                        chosen[end] = jnp.where(hit, 1.0, chosen[end])
                turner[which] = jnp.where(wanted == col, 1.0, 0.0).astype(BF16)
                for end in range(2):
                    chooser[which, end] = chosen[end].astype(BF16)

    def strip_arrivals(trip):
        @pl.when(rim)
        def _():
            @pl.when(corner)
            def _():
                here = seam[trip].at[0:6, 0:faces] if trip == 0 else seam[trip].at[0:6]
                pltpu.make_async_copy(here, here, seam_recv.at[trip]).wait()

            @pl.when(jnp.logical_not(corner))
            def _():
                here = seam[trip].at[0:7, 0:faces] if trip == 0 else seam[trip].at[0:7]
                pltpu.make_async_copy(here, here, seam_recv.at[trip]).wait()
        for which in range(2):
            active, edge, place, count, slot = rims[which]

            @pl.when(active)
            def _(which=which, edge=edge, place=place, count=count):
                part = place // (count // 2)
                lines = []
                for f in range(faces):
                    flip = flip_tab[edge, f]
                    lines.append(seam[trip][(part + flip * (1 - 2 * part)) * 4 + edge_tab[edge, f], face_tab[edge, f]])
                line = dot(turner[which], jnp.concatenate(lines, axis=0)).astype(BF16)
                strip_in[trip, edge] = line.reshape(faces, side, width)
                if trip == 0:
                    picked = dot(first_last, line).astype(BF16)
                    ends = [picked[:16], picked[16:]]
                else:
                    offered = jnp.concatenate(
                        [seam[trip][slot, faces + end] for slot in range(8) for end in range(2)], axis=0)
                    ends = [dot(chooser[which, end], offered).astype(BF16) for end in range(2)]
                for end in range(2):
                    end_src[trip, which, end] = ends[end]

                    @pl.when(place < count - 1 if end else place > 0)
                    def _(end=end):
                        end_copy(trip, which, end).start()
        for item in near:
            if item[3] < 4:
                @pl.when(item[2])
                def _(item=item):
                    near_arrival(trip, item[3]).wait()

    def corner_arrivals(trip):
        for v in range(2):
            for h in range(2):
                both = jnp.logical_and(bottom if v else top, right if h else left)

                @pl.when(jnp.logical_not(both))
                def _(v=v, h=h):
                    near_arrival(trip, 4 + 2 * v + h).wait()

                @pl.when(both)
                def _(v=v, h=h):
                    if trip == 0:
                        total = end_src[0, 0, h].astype(F32) + end_src[0, 1, v].astype(F32)
                        corner_in[0, 2 * v + h] = (0.5 * total).astype(BF16)
                    else:
                        corner_in[1, 2 * v + h] = jnp.zeros((16, width), BF16)

    load_x = pltpu.make_async_copy(x_hbm, xp.at[:, 1:side + 1], load_sem.at[0])
    load_w = pltpu.make_async_copy(w_hbm, w9, load_sem.at[1])
    load_c = pltpu.make_async_copy(cot_hbm, cot, load_sem.at[2])
    loads = [pltpu.make_async_copy(there, here, load_sem.at[3 + i]) for i, (there, here) in enumerate(
        ((face_hbm, face_tab), (edge_hbm, edge_tab), (flip_hbm, flip_tab), (bias_hbm, bias_ref)))]
    load_x.start()
    load_w.start()
    for load in loads:
        load.start()
    load_c.start()

    barrier = pltpu.get_barrier_semaphore()
    due = jnp.int32(0)

    def greet(on, tx, ty):
        @pl.when(on)
        def _():
            pl.semaphore_signal(barrier, inc=1, device_id=(tx, ty), device_id_type=MESH)
        return on.astype(jnp.int32)

    for which in range(2):
        for step, tx, ty, on in partners(which):
            due = due + greet(jnp.logical_and(on, jnp.logical_not(corner)) if which else on, tx, ty)
    for tx, ty, inside, slot, back in near:
        due = due + greet(inside, tx, ty)

    zero_rows = jnp.zeros((faces, side, width), BF16)
    xp[:, 0] = zero_rows
    xp[:, side + 1] = zero_rows
    sp[:, 0] = zero_rows
    sp[:, side + 1] = zero_rows
    load_x.wait()
    src[0, 0] = xp[:, 1]
    src[0, 1] = xp[:, side]
    column_pick = jnp.where(
        cols_iota((2 * side, cells)) == (rows_iota((2 * side, cells)) % side) * side
        + (rows_iota((2 * side, cells)) // side) * (side - 1), 1.0, 0.0).astype(BF16)
    for f in range(faces):
        both = dot(column_pick, xp[f, 1:side + 1].reshape(cells, width)).astype(BF16)
        src[0, 2, f] = both[:side]
        src[0, 3, f] = both[side:]
    for half in range(2):
        picked = dot(first_last, src[0, half].reshape(strip, width)).astype(BF16)
        corner_src[0, 2 * half] = picked[:16]
        corner_src[0, 2 * half + 1] = picked[16:]
    own_lines(0)
    pl.semaphore_wait(barrier, due)
    send_all(0)

    load_w.wait()
    for a in range(3):
        for b in range(3):
            tap = w9[a, b]
            back = tap.astype(F32).T.astype(BF16)
            wf[a * width:(a + 1) * width, b * width:(b + 1) * width] = tap
            vf[(2 - a) * width:(3 - a) * width, (2 - b) * width:(3 - b) * width] = back
            if b != 1:
                wcol[b // 2, :, a * width:(a + 1) * width] = tap
                vcol[b // 2, :, (2 - a) * width:(3 - a) * width] = back
    for load in loads:
        load.wait()
    prepare_choice()
    load_c.wait()
    for f in range(faces):
        both = dot(column_pick, cot[f].reshape(cells, width))
        colcot[0, f * side:(f + 1) * side] = both[:side]
        colcot[1, f * side:(f + 1) * side] = both[side:]

    def conv(source, f, weights):
        stacked = jnp.concatenate(
            [source[f, a:a + side].reshape(cells, width) for a in range(3)], axis=1)
        return shifted_sum(dot(stacked, weights), side)

    def forward_face(f, carry):
        acc[pl.ds(pl.multiple_of(f * cells, cells), cells)] = conv(xp, f, wf[...]) + bias_ref[...]
        return carry
    lax.fori_loop(0, faces, forward_face, 0)

    def add_strips(strips):
        for half in range(2):
            line = strips[half]
            for f in range(faces):
                at = f * cells + half * (cells - side)
                acc[at:at + side] += line[f * side:(f + 1) * side]
        for half in range(2):
            at = pl.ds(half * (side - 1), strip, stride=side)
            acc[at] = acc[at] + strips[2 + half]

    def add_corners(corners):
        for which in range(4):
            at = pl.ds((which // 2) * (cells - side) + (which % 2) * (side - 1), faces, stride=cells)
            acc[at] = acc[at] + corners[which]

    strip_arrivals(0)
    strips = []
    for edge in range(4):
        line = strip_in[0, edge].reshape(strip, width)
        weights = wf[2 * edge * width:(2 * edge + 1) * width] if edge < 2 else wcol[edge - 2]
        strips.append(shifted_sum(dot(line, weights), side))
    add_strips(strips)
    corner_arrivals(0)
    add_corners([dot(corner_in[0, 2 * a + b], w9[2 * a, 2 * b])[:faces] for a in range(2) for b in range(2)])

    rim_slopes = []
    for half in range(2):
        at = half * (cells - side)
        line = jnp.concatenate([acc[f * cells + at:f * cells + at + side] for f in range(faces)], axis=0)
        rim_slopes.append((cot[:, half * (side - 1)].reshape(strip, width).astype(F32) * silu_parts(line)[1]).astype(BF16))
    for half in range(2):
        line = acc[pl.ds(half * (side - 1), strip, stride=side)]
        rim_slopes.append((colcot[half] * silu_parts(line)[1]).astype(BF16))
    for edge in range(4):
        weights = vf[2 * (1 - edge) * width:(2 * (1 - edge) + 1) * width] if edge < 2 else vcol[edge - 2]
        ring[edge] = shifted_sum(dot(rim_slopes[edge], weights), side)
    for a in range(2):
        picked = dot(first_last, rim_slopes[a]).astype(BF16)
        for b in range(2):
            beyond = dot(picked[16 * b:16 * b + 16], vf[2 * (1 - a) * width:(2 * (1 - a) + 1) * width,
                                                        2 * (1 - b) * width:(2 * (1 - b) + 1) * width])
            corner_src[1, 2 * a + b] = beyond.astype(BF16)

            @pl.when(jnp.logical_and(bottom if a else top, right if b else left))
            def _(a=a, b=b, beyond=beyond):
                along_row = pl.ds(b * (side - 1), faces, stride=side)
                along_col = pl.ds(a * (side - 1), faces, stride=side)
                ring[a, along_row] = ring[a, along_row] + 0.5 * beyond[:faces]
                ring[2 + b, along_col] = ring[2 + b, along_col] + 0.5 * beyond[:faces]
    for edge in range(4):
        src[1, edge] = ring[edge].astype(BF16).reshape(faces, side, width)
    own_lines(1)
    send_all(1)

    def adjoint_face(f, carry):
        at = pl.ds(pl.multiple_of(f * cells, cells), cells)
        value, slope = silu_parts(acc[at])
        act[f] = value.astype(BF16).reshape(side, side, width)
        slope = cot[f].reshape(cells, width).astype(F32) * slope
        sp[f, 1:side + 1] = slope.astype(BF16).reshape(side, side, width)
        acc[at] = conv(sp, f, vf[...])
        return carry
    lax.fori_loop(0, faces, adjoint_face, 0)

    strip_arrivals(1)
    add_strips([strip_in[1, edge].reshape(strip, width).astype(F32) for edge in range(4)])
    corner_arrivals(1)
    add_corners([corner_in[1, which].astype(F32)[:faces] for which in range(4)])

    def finish_face(f, carry):
        at = pl.ds(pl.multiple_of(f * cells, cells), cells)
        grad[f] = acc[at].astype(BF16).reshape(side, side, width)
        return carry
    lax.fori_loop(0, faces, finish_face, 0)
    wait_sent(0)
    wait_sent(1)


def shards(features, weight, out_bias, cotangent, seam_face, seam_edge, seam_flip):
    faces, side, _, width = features.shape
    nx, ny = lax.axis_size("fx"), lax.axis_size("fy")
    patch = (faces, side, side, width)
    padded = (faces, side + 2, side, width)
    strip = faces * side
    dma = pltpu.SemaphoreType.DMA
    hbm = pl.BlockSpec(memory_space=pltpu.HBM)
    vmem = pl.BlockSpec(memory_space=pltpu.VMEM)
    return pl.pallas_call(
        functools.partial(kernel, nx, ny, faces, side, width),
        out_shape=(jax.ShapeDtypeStruct(patch, BF16), jax.ShapeDtypeStruct(patch, BF16)),
        in_specs=[hbm] * 7,
        out_specs=(vmem, vmem),
        scratch_shapes=[
            pltpu.SMEM((4, faces), jnp.int32),
            pltpu.SMEM((4, faces), jnp.int32),
            pltpu.SMEM((4, faces), jnp.int32),
            pltpu.VMEM((1, width), F32),
            pltpu.VMEM(padded, BF16),
            pltpu.VMEM(patch, BF16),
            pltpu.VMEM((3, 3, width, width), BF16),
            pltpu.VMEM((faces * side * side, width), F32),
            pltpu.VMEM(padded, BF16),
            pltpu.VMEM((3 * width, 3 * width), BF16),
            pltpu.VMEM((2, width, 3 * width), BF16),
            pltpu.VMEM((3 * width, 3 * width), BF16),
            pltpu.VMEM((2, width, 3 * width), BF16),
            pltpu.VMEM((2, strip, width), F32),
            pltpu.VMEM((4, strip, width), F32),
            pltpu.VMEM((2, strip, strip), BF16),
            pltpu.VMEM((2, 2, 16, 256), BF16),
            pltpu.VMEM((2, 4, faces, side, width), BF16),
            pltpu.VMEM((2, 4, 16, width), BF16),
            pltpu.VMEM((2, 4, faces, side, width), BF16),
            pltpu.VMEM((2, 4, 16, width), BF16),
            pltpu.VMEM((8, faces + 2, side, width), BF16),
            pltpu.VMEM((8, faces + 2, side, width), BF16),
            pltpu.VMEM((2, 2, 2, 16, width), BF16),
            dma((2, 8)),
            dma((2, 8)),
            dma((2, 2, 8)),
            dma((2,)),
            dma((2, 2, 2)),
            dma((7,)),
        ],
        compiler_params=pltpu.CompilerParams(
            collective_id=0, has_side_effects=True, vmem_limit_bytes=40 * 1024 * 1024),
    )(*[pltpu.with_memory_space_constraint(value, pltpu.HBM) for value in (
        seam_face.T, seam_edge.T, seam_flip.T, out_bias.reshape(1, width), features, weight, cotangent)])


def solution(mesh):
    in_specs = (P(None, "fx", "fy", None), P(), P(), P(None, "fx", "fy", None), P(), P(), P())
    out_specs = (P(None, "fx", "fy", None), P(None, "fx", "fy", None))
    return jax.shard_map(shards, mesh=mesh, in_specs=in_specs, out_specs=out_specs, check_vma=False)
```

time: 59.2 us -> 44.9 us (0.76)
  the two profiles are of different devices: /device:TPU:57 before, /device:TPU:2 now
where the time goes in v2:
time: 44.9 us; the launch traced here: 44.8 us
  Pallas kernels  42.4 us (94%)
  local copies, waits for them, and re-layouts  1.76 us (4%)
  between operations  0.64 us (1%)
    pallas_call x1, Pallas kernels, shards(): pl.pallas_call(functools.partial(kernel, nx, ny, faces, side, width), out...  42.4 us
    unnamed x2, local copies, waits for them, and re-layouts  1.76 us

profile of v2, /device:TPU:2, one launch (start us, length us, event | category | flops | bytes accessed | tf_op | source)
XLA Modules:
  0.0 44.8 jit_solution(12468087556659446920)
XLA Ops:
  0.6 42.4 %shard_map.86 = (bf16[12,16,16,128]{3,2,1,0:T(8,128)(2,1)S(1)}, bf16[12,16,16,128]{3,2,1,0:T(8,128)(2,1)S(1)}) custom-call(s32[4,12]{1,0:T(4,128)} %bitcast.4, s32[4,12]{1,0:T(4,128)} %bitcast.5, s32[4,12]{1,0:T(4,128)} %bitcast.6, f32[1,128]{1,0:T(1,128)} %bitcast.7, bf16[12,16,16,128]{3,2,1,0:T(8,128)(2,1)} %x_hbm.1, bf16[3,3,128,128]{3,2,1,0:T(8,128)(2,1)} %w_hbm.1, ...), custom_call_target="tpu_custom_call" | custom-call | tf_op jit(solution)/shard_map/pallas_call | solution.py:412
  43.0 0.9 %copy.11 = bf16[12,16,16,128]{3,2,1,0:T(8,128)(2,1)} copy(bf16[12,16,16,128]{3,2,1,0:T(8,128)(2,1)S(1)} %get-tuple-element.4) | data formatting | bytes 1572864
  43.9 0.9 %copy.12 = bf16[12,16,16,128]{3,2,1,0:T(8,128)(2,1)} copy(bf16[12,16,16,128]{3,2,1,0:T(8,128)(2,1)S(1)} %get-tuple-element.5) | data formatting | bytes 1572864

commit v3 on v2

--- a/solution.py
+++ b/solution.py
@@ -41,12 +41,13 @@
            face_hbm, edge_hbm, flip_hbm, bias_hbm, x_hbm, w_hbm, cot_hbm,
            act, grad,
            face_tab, edge_tab, flip_tab, bias_ref, xp, cot, w9, acc, sp,
-           wf, wcol, vf, vcol, colcot, ring, turner, chooser,
-           src, corner_src, strip_in, corner_in, seam_first, seam_second, end_src,
-           near_send, near_recv, seam_send, seam_recv, ends_send, load_sem):
+           wf, wcol, vf, vcol, colcot, ring, turner, chooser, end_cells,
+           src, corner_src, strip_in, corner_in, seam_first, seam_second,
+           near_send, near_recv, seam_send, seam_recv, tail_send, relay_send, ends_send, ends_recv, load_sem):
     x = lax.axis_index("fx")
     y = lax.axis_index("fy")
     top, bottom, left, right = x == 0, x == nx - 1, y == 0, y == ny - 1
+    on_rim = (top, bottom, left, right)
     row_rim = jnp.logical_or(top, bottom)
     col_rim = jnp.logical_or(left, right)
     rim = jnp.logical_or(row_rim, col_rim)
@@ -54,6 +55,7 @@
     seam = (seam_first, seam_second)
     cells = side * side
     strip = faces * side
+    last_row = cells - side
     row_edge = x // (nx - 1)
     col_edge = 2 + y // (ny - 1)
     rims = ((row_rim, row_edge, y, ny, (y // (ny // 2)) * 4 + row_edge),
@@ -68,7 +70,7 @@
         back = slot ^ 1 if slot < 4 else 4 + (3 - (slot - 4))
         near.append((tx, ty, inside, slot, back))
 
-    def partners(which):
+    def partners(which, tail=True):
         active, edge, place, count, slot = rims[which]
         for kind in range(2):
             for half in range(2):
@@ -79,6 +81,9 @@
                     on = jnp.logical_and(active, other)
                     if kind == 1:
                         on = jnp.logical_and(on, jnp.logical_not(corner))
+                    by_relay = which == 0 and kind == 0 and turn == 1
+                    if by_relay and not tail:
+                        on = jnp.logical_and(on, jnp.logical_or(corner, half == row_edge))
                     yield kind * 4 + half * 2 + turn, tx, ty, on
 
     def near_copy(trip, item):
@@ -95,47 +100,104 @@
         here = strip_in.at[trip, slot] if slot < 4 else corner_in.at[trip, slot - 4]
         return pltpu.make_async_copy(here, here, near_recv.at[trip, slot])
 
-    def seam_copy(trip, which, step, tx, ty):
+    def end_spot(which, edge, end):
+        return 2 * edge + end if which == 0 else edge - 2 + 2 * end
+
+    def has_next(which, end):
+        place, count = rims[which][2], rims[which][3]
+        return place < count - 1 if end else place > 0
+
+    def seam_copy(trip, which, step, tx, ty, tail):
         slot = rims[which][4]
-        line = seam[trip].at[slot, 0:faces] if trip == 0 else seam[trip].at[slot]
+        line = seam[trip].at[slot, faces:faces + 2] if tail else seam[trip].at[slot, 0:faces]
+        sems = tail_send if tail else seam_send
+        straight = which == 0 and not tail and step < 4 and step % 2 == 0
+        arrived = seam_recv.at[trip, 1 if tail else 0]
+        if straight:
+            arrived = seam_recv.at[trip, 2 * jnp.logical_not(corner).astype(jnp.int32)]
         return pltpu.make_async_remote_copy(
-            src_ref=line, dst_ref=line, send_sem=seam_send.at[trip, which, step],
-            recv_sem=seam_recv.at[trip], device_id=(tx, ty), device_id_type=MESH)
+            src_ref=line, dst_ref=line, send_sem=sems.at[trip, which, step],
+            recv_sem=arrived, device_id=(tx, ty), device_id_type=MESH)
+
+    relays = jnp.logical_and(row_rim, jnp.logical_not(corner))
+
+    def relay_line(trip):
+        return seam[trip].at[(y // (ny // 2)) * 4 + 1 - row_edge, 0:faces]
+
+    def relay_copy(trip):
+        line = relay_line(trip)
+        return pltpu.make_async_remote_copy(
+            src_ref=line, dst_ref=line, send_sem=relay_send.at[trip],
+            recv_sem=seam_recv.at[trip, 0], device_id=(x, ny - 1 - y), device_id_type=MESH)
+
+    def send_relay(trip):
+        @pl.when(relays)
+        def _():
+            line = relay_line(trip)
+            pltpu.make_async_copy(line, line, seam_recv.at[trip, 2]).wait()
+            relay_copy(trip).start()
 
     def end_copy(trip, which, end):
         active, edge, place, count, slot = rims[which]
         spot = place + 2 * end - 1
-        if which == 0:
-            tx, ty, back = x, spot, 2 * edge + 1 - end
-        else:
-            tx, ty, back = spot, y, edge - 2 + 2 * (1 - end)
+        tx, ty = (x, spot) if which == 0 else (spot, y)
         return pltpu.make_async_remote_copy(
-            src_ref=end_src.at[trip, which, end], dst_ref=corner_in.at[trip, back],
-            send_sem=ends_send.at[trip, which, end], recv_sem=near_recv.at[trip, 4 + back],
+            src_ref=corner_src.at[trip, end_spot(which, edge, end)],
+            dst_ref=seam[trip].at[(spot // (count // 2)) * 4 + edge, faces + 1 - end],
+            send_sem=ends_send.at[trip, which, end], recv_sem=ends_recv.at[trip, which, 1 - end],
             device_id=(tx, ty), device_id_type=MESH)
 
-    def send_all(trip):
+    def send_line(trip, which):
+        active = rims[which][0]
+        for end in range(2):
+            @pl.when(jnp.logical_and(active, has_next(which, end)))
+            def _(end=end):
+                end_copy(trip, which, end).start()
+        for step, tx, ty, on in partners(which, False):
+            @pl.when(on)
+            def _(step=step, tx=tx, ty=ty):
+                seam_copy(trip, which, step, tx, ty, False).start()
+
+    def send_tails(trip):
         for which in range(2):
+            active, edge, place, count, slot = rims[which]
+            for end in range(2):
+                @pl.when(jnp.logical_and(active, has_next(which, end)))
+                def _(which=which, end=end, slot=slot):
+                    here = seam[trip].at[slot, faces + end]
+                    pltpu.make_async_copy(here, here, ends_recv.at[trip, which, end]).wait()
             for step, tx, ty, on in partners(which):
                 @pl.when(on)
                 def _(which=which, step=step, tx=tx, ty=ty):
-                    seam_copy(trip, which, step, tx, ty).start()
+                    seam_copy(trip, which, step, tx, ty, True).start()
+
+    def send_near(trip, slots):
         for item in near:
-            @pl.when(item[2])
-            def _(item=item):
-                near_copy(trip, item).start()
+            if item[3] in slots:
+                @pl.when(item[2])
+                def _(item=item):
+                    near_copy(trip, item).start()
 
     def wait_sent(trip):
-        for which in range(2):
-            for step, tx, ty, on in partners(which):
-                @pl.when(on)
-                def _(which=which, step=step, tx=tx, ty=ty):
-                    seam_copy(trip, which, step, tx, ty).wait_send()
-            active, edge, place, count, slot = rims[which]
-            for end in range(2):
-                @pl.when(jnp.logical_and(active, place < count - 1 if end else place > 0))
-                def _(which=which, end=end):
-                    end_copy(trip, which, end).wait_send()
+        @pl.when(rim)
+        def _():
+            for which in range(2):
+                active = rims[which][0]
+                for step, tx, ty, on in partners(which, False):
+                    @pl.when(on)
+                    def _(which=which, step=step, tx=tx, ty=ty):
+                        seam_copy(trip, which, step, tx, ty, False).wait_send()
+                for step, tx, ty, on in partners(which):
+                    @pl.when(on)
+                    def _(which=which, step=step, tx=tx, ty=ty):
+                        seam_copy(trip, which, step, tx, ty, True).wait_send()
+                for end in range(2):
+                    @pl.when(jnp.logical_and(active, has_next(which, end)))
+                    def _(which=which, end=end):
+                        end_copy(trip, which, end).wait_send()
+        @pl.when(relays)
+        def _():
+            relay_copy(trip).wait_send()
         for item in near:
             @pl.when(item[2])
             def _(item=item):
@@ -146,18 +208,6 @@
             cols_iota((32, strip)) == (rows_iota((32, strip)) % 16) * side + (rows_iota((32, strip)) // 16) * (side - 1),
             rows_iota((32, strip)) % 16 < faces),
         1.0, 0.0).astype(BF16)
-
-    def own_lines(trip):
-        for which in range(2):
-            active, edge, place, count, slot = rims[which]
-
-            @pl.when(active)
-            def _(which=which, edge=edge, slot=slot):
-                seam[trip][slot, 0:faces] = src[trip, edge]
-                if trip == 1:
-                    for end in range(2):
-                        at = 2 * edge + end if which == 0 else edge - 2 + 2 * end
-                        seam[trip][slot, faces + end] = corner_src[trip, at]
 
     def prepare_choice():
         for which in range(2):
@@ -184,18 +234,24 @@
                 for end in range(2):
                     chooser[which, end] = chosen[end].astype(BF16)
 
-    def strip_arrivals(trip):
-        @pl.when(rim)
-        def _():
-            @pl.when(corner)
-            def _():
-                here = seam[trip].at[0:6, 0:faces] if trip == 0 else seam[trip].at[0:6]
-                pltpu.make_async_copy(here, here, seam_recv.at[trip]).wait()
-
-            @pl.when(jnp.logical_not(corner))
-            def _():
-                here = seam[trip].at[0:7, 0:faces] if trip == 0 else seam[trip].at[0:7]
-                pltpu.make_async_copy(here, here, seam_recv.at[trip]).wait()
+    def seam_arrivals(trip):
+        def wait_for(lines, tails):
+            here = seam[trip].at[0:lines, 0:faces]
+            pltpu.make_async_copy(here, here, seam_recv.at[trip, 0]).wait()
+            here = seam[trip].at[0:tails, 0:2]
+            pltpu.make_async_copy(here, here, seam_recv.at[trip, 1]).wait()
+
+        @pl.when(corner)
+        def _():
+            wait_for(6, 6)
+
+        @pl.when(relays)
+        def _():
+            wait_for(6, 7)
+
+        @pl.when(jnp.logical_not(row_rim))
+        def _():
+            wait_for(7, 7)
         for which in range(2):
             active, edge, place, count, slot = rims[which]
 
@@ -209,40 +265,17 @@
                 line = dot(turner[which], jnp.concatenate(lines, axis=0)).astype(BF16)
                 strip_in[trip, edge] = line.reshape(faces, side, width)
                 if trip == 0:
-                    picked = dot(first_last, line).astype(BF16)
-                    ends = [picked[:16], picked[16:]]
-                else:
-                    offered = jnp.concatenate(
-                        [seam[trip][slot, faces + end] for slot in range(8) for end in range(2)], axis=0)
-                    ends = [dot(chooser[which, end], offered).astype(BF16) for end in range(2)]
+                    @pl.when(corner)
+                    def _():
+                        end_cells[which] = dot(first_last, line)
+                offered = jnp.concatenate(
+                    [seam[trip][slot, faces + end] for slot in range(8) for end in range(2)], axis=0)
                 for end in range(2):
-                    end_src[trip, which, end] = ends[end]
-
-                    @pl.when(place < count - 1 if end else place > 0)
-                    def _(end=end):
-                        end_copy(trip, which, end).start()
-        for item in near:
-            if item[3] < 4:
-                @pl.when(item[2])
-                def _(item=item):
-                    near_arrival(trip, item[3]).wait()
-
-    def corner_arrivals(trip):
-        for v in range(2):
-            for h in range(2):
-                both = jnp.logical_and(bottom if v else top, right if h else left)
-
-                @pl.when(jnp.logical_not(both))
-                def _(v=v, h=h):
-                    near_arrival(trip, 4 + 2 * v + h).wait()
-
-                @pl.when(both)
-                def _(v=v, h=h):
-                    if trip == 0:
-                        total = end_src[0, 0, h].astype(F32) + end_src[0, 1, v].astype(F32)
-                        corner_in[0, 2 * v + h] = (0.5 * total).astype(BF16)
-                    else:
-                        corner_in[1, 2 * v + h] = jnp.zeros((16, width), BF16)
+                    value = dot(chooser[which, end], offered).astype(BF16)
+
+                    @pl.when(has_next(which, end))
+                    def _(end=end, value=value):
+                        corner_in[trip, end_spot(which, edge, end)] = value
 
     load_x = pltpu.make_async_copy(x_hbm, xp.at[:, 1:side + 1], load_sem.at[0])
     load_w = pltpu.make_async_copy(w_hbm, w9, load_sem.at[1])
@@ -271,13 +304,31 @@
         due = due + greet(inside, tx, ty)
 
     zero_rows = jnp.zeros((faces, side, width), BF16)
+    zero_tile = jnp.zeros((side, width), BF16)
     xp[:, 0] = zero_rows
     xp[:, side + 1] = zero_rows
     sp[:, 0] = zero_rows
     sp[:, side + 1] = zero_rows
+    for which in range(2):
+        for end in range(2):
+            @pl.when(jnp.logical_and(rims[which][0], jnp.logical_not(has_next(which, end))))
+            def _(which=which, end=end):
+                for trip in range(2):
+                    seam[trip][rims[which][4], faces + end] = zero_tile
     load_x.wait()
-    src[0, 0] = xp[:, 1]
-    src[0, 1] = xp[:, side]
+    for half in range(2):
+        line = xp[:, 1 + half * (side - 1)]
+        src[0, half] = line
+        picked = dot(first_last, line.reshape(strip, width)).astype(BF16)
+        corner_src[0, 2 * half] = picked[:16]
+        corner_src[0, 2 * half + 1] = picked[16:]
+
+        @pl.when(on_rim[half])
+        def _(line=line):
+            seam[0][rims[0][4], 0:faces] = line
+    pl.semaphore_wait(barrier, due)
+    send_line(0, 0)
+    send_near(0, (0, 1, 4, 5, 6, 7))
     column_pick = jnp.where(
         cols_iota((2 * side, cells)) == (rows_iota((2 * side, cells)) % side) * side
         + (rows_iota((2 * side, cells)) // side) * (side - 1), 1.0, 0.0).astype(BF16)
@@ -285,13 +336,14 @@
         both = dot(column_pick, xp[f, 1:side + 1].reshape(cells, width)).astype(BF16)
         src[0, 2, f] = both[:side]
         src[0, 3, f] = both[side:]
-    for half in range(2):
-        picked = dot(first_last, src[0, half].reshape(strip, width)).astype(BF16)
-        corner_src[0, 2 * half] = picked[:16]
-        corner_src[0, 2 * half + 1] = picked[16:]
-    own_lines(0)
-    pl.semaphore_wait(barrier, due)
-    send_all(0)
+
+    @pl.when(col_rim)
+    def _():
+        seam[0][rims[1][4], 0:faces] = src[0, col_edge]
+    send_line(0, 1)
+    send_near(0, (2, 3))
+    send_tails(0)
+    send_relay(0)
 
     load_w.wait()
     for a in range(3):
@@ -322,59 +374,111 @@
         return carry
     lax.fori_loop(0, faces, forward_face, 0)
 
-    def add_strips(strips):
-        for half in range(2):
-            line = strips[half]
+    def add_strip(edge, value):
+        if edge < 2:
             for f in range(faces):
-                at = f * cells + half * (cells - side)
-                acc[at:at + side] += line[f * side:(f + 1) * side]
-        for half in range(2):
-            at = pl.ds(half * (side - 1), strip, stride=side)
-            acc[at] = acc[at] + strips[2 + half]
-
-    def add_corners(corners):
-        for which in range(4):
-            at = pl.ds((which // 2) * (cells - side) + (which % 2) * (side - 1), faces, stride=cells)
-            acc[at] = acc[at] + corners[which]
-
-    strip_arrivals(0)
-    strips = []
-    for edge in range(4):
+                at = f * cells + edge * last_row
+                acc[at:at + side] += value[f * side:(f + 1) * side]
+        else:
+            at = pl.ds((edge - 2) * (side - 1), strip, stride=side)
+            acc[at] = acc[at] + value
+
+    def corner_at(v, h):
+        return pl.ds(v * last_row + h * (side - 1), faces, stride=cells)
+
+    def add_corner(v, h, value):
+        acc[corner_at(v, h)] = acc[corner_at(v, h)] + value
+
+    def forward_strip(edge):
         line = strip_in[0, edge].reshape(strip, width)
         weights = wf[2 * edge * width:(2 * edge + 1) * width] if edge < 2 else wcol[edge - 2]
-        strips.append(shifted_sum(dot(line, weights), side))
-    add_strips(strips)
-    corner_arrivals(0)
-    add_corners([dot(corner_in[0, 2 * a + b], w9[2 * a, 2 * b])[:faces] for a in range(2) for b in range(2)])
-
-    rim_slopes = []
-    for half in range(2):
-        at = half * (cells - side)
-        line = jnp.concatenate([acc[f * cells + at:f * cells + at + side] for f in range(faces)], axis=0)
-        rim_slopes.append((cot[:, half * (side - 1)].reshape(strip, width).astype(F32) * silu_parts(line)[1]).astype(BF16))
-    for half in range(2):
-        line = acc[pl.ds(half * (side - 1), strip, stride=side)]
-        rim_slopes.append((colcot[half] * silu_parts(line)[1]).astype(BF16))
+        add_strip(edge, shifted_sum(dot(line, weights), side))
+
+    def forward_corner(v, h):
+        add_corner(v, h, dot(corner_in[0, 2 * v + h], w9[2 * v, 2 * h])[:faces])
+
+    def from_near(trip, strip_step, corner_step):
+        for item in near:
+            @pl.when(item[2])
+            def _(item=item):
+                near_arrival(trip, item[3]).wait()
+                if item[3] < 4:
+                    strip_step(item[3])
+                else:
+                    corner_step((item[3] - 4) // 2, item[3] % 2)
+
+    corner_pairs = [(v, h) for v in range(2) for h in range(2)]
+
+    def at_both(v, h):
+        return jnp.logical_and(bottom if v else top, right if h else left)
+
+    from_near(0, forward_strip, forward_corner)
+
+    @pl.when(rim)
+    def _():
+        seam_arrivals(0)
+        for v, h in corner_pairs:
+            @pl.when(at_both(v, h))
+            def _(v=v, h=h):
+                total = end_cells[0, 16 * h:16 * h + 16] + end_cells[1, 16 * v:16 * v + 16]
+                corner_in[0, 2 * v + h] = (0.5 * total).astype(BF16)
+        for edge in range(4):
+            @pl.when(on_rim[edge])
+            def _(edge=edge):
+                forward_strip(edge)
+        for v, h in corner_pairs:
+            @pl.when(jnp.logical_or(bottom if v else top, right if h else left))
+            def _(v=v, h=h):
+                forward_corner(v, h)
+
+    def ring_strip(edge):
+        if edge < 2:
+            at = edge * last_row
+            line = jnp.concatenate([acc[f * cells + at:f * cells + at + side] for f in range(faces)], axis=0)
+            turned_cot = cot[:, edge * (side - 1)].reshape(strip, width).astype(F32)
+            weights = vf[2 * (1 - edge) * width:(2 * (1 - edge) + 1) * width]
+        else:
+            line = acc[pl.ds((edge - 2) * (side - 1), strip, stride=side)]
+            turned_cot = colcot[edge - 2]
+            weights = vcol[edge - 2]
+        slope = (turned_cot * silu_parts(line)[1]).astype(BF16)
+        return shifted_sum(dot(slope, weights), side)
+
+    beyond = []
+    for v, h in corner_pairs:
+        slope = colcot.at[h][pl.ds(v * (side - 1), faces, stride=side)] * silu_parts(acc[corner_at(v, h)])[1]
+        slope = jnp.concatenate([slope, jnp.zeros((16 - faces, width), F32)], axis=0).astype(BF16)
+        value = dot(slope, vf[2 * (1 - v) * width:(2 * (1 - v) + 1) * width, 2 * (1 - h) * width:(2 * (1 - h) + 1) * width])
+        beyond.append(value)
+        corner_src[1, 2 * v + h] = value.astype(BF16)
+
+    @pl.when(rim)
+    def _():
+        for edge in range(4):
+            @pl.when(on_rim[edge])
+            def _(edge=edge):
+                ring[edge] = ring_strip(edge)
+        for v, h in corner_pairs:
+            @pl.when(at_both(v, h))
+            def _(v=v, h=h):
+                along_row = pl.ds(h * (side - 1), faces, stride=side)
+                along_col = pl.ds(v * (side - 1), faces, stride=side)
+                ring[v, along_row] = ring[v, along_row] + 0.5 * beyond[2 * v + h][:faces]
+                ring[2 + h, along_col] = ring[2 + h, along_col] + 0.5 * beyond[2 * v + h][:faces]
+        for which in range(2):
+            active, edge, place, count, slot = rims[which]
+
+            @pl.when(active)
+            def _(edge=edge, slot=slot):
+                seam[1][slot, 0:faces] = ring[edge].astype(BF16).reshape(faces, side, width)
+            send_line(1, which)
     for edge in range(4):
-        weights = vf[2 * (1 - edge) * width:(2 * (1 - edge) + 1) * width] if edge < 2 else vcol[edge - 2]
-        ring[edge] = shifted_sum(dot(rim_slopes[edge], weights), side)
-    for a in range(2):
-        picked = dot(first_last, rim_slopes[a]).astype(BF16)
-        for b in range(2):
-            beyond = dot(picked[16 * b:16 * b + 16], vf[2 * (1 - a) * width:(2 * (1 - a) + 1) * width,
-                                                        2 * (1 - b) * width:(2 * (1 - b) + 1) * width])
-            corner_src[1, 2 * a + b] = beyond.astype(BF16)
-
-            @pl.when(jnp.logical_and(bottom if a else top, right if b else left))
-            def _(a=a, b=b, beyond=beyond):
-                along_row = pl.ds(b * (side - 1), faces, stride=side)
-                along_col = pl.ds(a * (side - 1), faces, stride=side)
-                ring[a, along_row] = ring[a, along_row] + 0.5 * beyond[:faces]
-                ring[2 + b, along_col] = ring[2 + b, along_col] + 0.5 * beyond[:faces]
-    for edge in range(4):
-        src[1, edge] = ring[edge].astype(BF16).reshape(faces, side, width)
-    own_lines(1)
-    send_all(1)
+        @pl.when(jnp.logical_not(on_rim[edge]))
+        def _(edge=edge):
+            src[1, edge] = ring_strip(edge).astype(BF16).reshape(faces, side, width)
+    send_near(1, range(8))
+    send_tails(1)
+    send_relay(1)
 
     def adjoint_face(f, carry):
         at = pl.ds(pl.multiple_of(f * cells, cells), cells)
@@ -386,18 +490,48 @@
         return carry
     lax.fori_loop(0, faces, adjoint_face, 0)
 
-    strip_arrivals(1)
-    add_strips([strip_in[1, edge].reshape(strip, width).astype(F32) for edge in range(4)])
-    corner_arrivals(1)
-    add_corners([corner_in[1, which].astype(F32)[:faces] for which in range(4)])
+    def adjoint_strip(edge):
+        add_strip(edge, strip_in[1, edge].reshape(strip, width).astype(F32))
+
+    def adjoint_corner(v, h):
+        add_corner(v, h, corner_in[1, 2 * v + h].astype(F32)[:faces])
 
     def finish_face(f, carry):
         at = pl.ds(pl.multiple_of(f * cells, cells), cells)
         grad[f] = acc[at].astype(BF16).reshape(side, side, width)
         return carry
-    lax.fori_loop(0, faces, finish_face, 0)
+
     wait_sent(0)
+    from_near(1, adjoint_strip, adjoint_corner)
+
+    @pl.when(jnp.logical_not(col_rim))
+    def _():
+        lax.fori_loop(0, faces, finish_face, 0)
     wait_sent(1)
+
+    @pl.when(rim)
+    def _():
+        seam_arrivals(1)
+        for edge in range(4):
+            @pl.when(on_rim[edge])
+            def _(edge=edge):
+                adjoint_strip(edge)
+        for v, h in corner_pairs:
+            vertical, horizontal = bottom if v else top, right if h else left
+
+            @pl.when(vertical != horizontal)
+            def _(v=v, h=h):
+                adjoint_corner(v, h)
+
+        @pl.when(col_rim)
+        def _():
+            lax.fori_loop(0, faces, finish_face, 0)
+        for edge in range(2):
+            @pl.when(jnp.logical_and(on_rim[edge], jnp.logical_not(col_rim)))
+            def _(edge=edge):
+                for f in range(faces):
+                    at = f * cells + edge * last_row
+                    grad[f, edge * (side - 1)] = acc[at:at + side].astype(BF16)
 
 
 def shards(features, weight, out_bias, cotangent, seam_face, seam_edge, seam_flip):
@@ -432,17 +566,20 @@
             pltpu.VMEM((4, strip, width), F32),
             pltpu.VMEM((2, strip, strip), BF16),
             pltpu.VMEM((2, 2, 16, 256), BF16),
+            pltpu.VMEM((2, 32, width), F32),
             pltpu.VMEM((2, 4, faces, side, width), BF16),
             pltpu.VMEM((2, 4, 16, width), BF16),
             pltpu.VMEM((2, 4, faces, side, width), BF16),
             pltpu.VMEM((2, 4, 16, width), BF16),
             pltpu.VMEM((8, faces + 2, side, width), BF16),
             pltpu.VMEM((8, faces + 2, side, width), BF16),
-            pltpu.VMEM((2, 2, 2, 16, width), BF16),
             dma((2, 8)),
             dma((2, 8)),
             dma((2, 2, 8)),
+            dma((2, 3)),
+            dma((2, 2, 8)),
             dma((2,)),
+            dma((2, 2, 2)),
             dma((2, 2, 2)),
             dma((7,)),
         ],

time: 44.9 us -> 41.8 us (0.931)
  the two profiles are of different devices: /device:TPU:2 before, /device:TPU:57 now
where the time goes in v3:
time: 41.8 us; the launch traced here: 41.6 us
  Pallas kernels  39.2 us (94%)
  local copies, waits for them, and re-layouts  1.76 us (4%)
  between operations  0.64 us (2%)
    pallas_call x1, Pallas kernels, shards(): pl.pallas_call(functools.partial(kernel, nx, ny, faces, side, width), out...  39.2 us
    unnamed x2, local copies, waits for them, and re-layouts  1.76 us

profile of v3, /device:TPU:57, one launch (start us, length us, event | category | flops | bytes accessed | tf_op | source)
XLA Modules:
  0.0 41.6 jit_solution(16005090699652780562)
XLA Ops:
  0.6 39.2 %shard_map.86 = (bf16[12,16,16,128]{3,2,1,0:T(8,128)(2,1)S(1)}, bf16[12,16,16,128]{3,2,1,0:T(8,128)(2,1)S(1)}) custom-call(s32[4,12]{1,0:T(4,128)} %bitcast.4, s32[4,12]{1,0:T(4,128)} %bitcast.5, s32[4,12]{1,0:T(4,128)} %bitcast.6, f32[1,128]{1,0:T(1,128)} %bitcast.7, bf16[12,16,16,128]{3,2,1,0:T(8,128)(2,1)} %x_hbm.1, bf16[3,3,128,128]{3,2,1,0:T(8,128)(2,1)} %w_hbm.1, ...), custom_call_target="tpu_custom_call" | custom-call | tf_op jit(solution)/shard_map/pallas_call | solution.py:546
  39.9 0.9 %copy.11 = bf16[12,16,16,128]{3,2,1,0:T(8,128)(2,1)} copy(bf16[12,16,16,128]{3,2,1,0:T(8,128)(2,1)S(1)} %get-tuple-element.4) | data formatting | bytes 1572864
  40.8 0.9 %copy.12 = bf16[12,16,16,128]{3,2,1,0:T(8,128)(2,1)} copy(bf16[12,16,16,128]{3,2,1,0:T(8,128)(2,1)S(1)} %get-tuple-element.5) | data formatting | bytes 1572864

commit v4 on v3

--- a/solution.py
+++ b/solution.py
@@ -147,12 +147,13 @@
             send_sem=ends_send.at[trip, which, end], recv_sem=ends_recv.at[trip, which, 1 - end],
             device_id=(tx, ty), device_id_type=MESH)
 
-    def send_line(trip, which):
-        active = rims[which][0]
+    def send_ends(trip, which):
         for end in range(2):
-            @pl.when(jnp.logical_and(active, has_next(which, end)))
+            @pl.when(jnp.logical_and(rims[which][0], has_next(which, end)))
             def _(end=end):
                 end_copy(trip, which, end).start()
+
+    def send_line(trip, which):
         for step, tx, ty, on in partners(which, False):
             @pl.when(on)
             def _(step=step, tx=tx, ty=ty):
@@ -282,6 +283,10 @@
     load_c = pltpu.make_async_copy(cot_hbm, cot, load_sem.at[2])
     loads = [pltpu.make_async_copy(there, here, load_sem.at[3 + i]) for i, (there, here) in enumerate(
         ((face_hbm, face_tab), (edge_hbm, edge_tab), (flip_hbm, flip_tab), (bias_hbm, bias_ref)))]
+    load_rows = [pltpu.make_async_copy(x_hbm.at[:, half * (side - 1)], src.at[0, half], load_sem.at[7 + half])
+                 for half in range(2)]
+    for load in load_rows:
+        load.start()
     load_x.start()
     load_w.start()
     for load in loads:
@@ -305,20 +310,15 @@
 
     zero_rows = jnp.zeros((faces, side, width), BF16)
     zero_tile = jnp.zeros((side, width), BF16)
-    xp[:, 0] = zero_rows
-    xp[:, side + 1] = zero_rows
-    sp[:, 0] = zero_rows
-    sp[:, side + 1] = zero_rows
     for which in range(2):
         for end in range(2):
             @pl.when(jnp.logical_and(rims[which][0], jnp.logical_not(has_next(which, end))))
             def _(which=which, end=end):
                 for trip in range(2):
                     seam[trip][rims[which][4], faces + end] = zero_tile
-    load_x.wait()
     for half in range(2):
-        line = xp[:, 1 + half * (side - 1)]
-        src[0, half] = line
+        load_rows[half].wait()
+        line = src[0, half]
         picked = dot(first_last, line.reshape(strip, width)).astype(BF16)
         corner_src[0, 2 * half] = picked[:16]
         corner_src[0, 2 * half + 1] = picked[16:]
@@ -327,8 +327,11 @@
         def _(line=line):
             seam[0][rims[0][4], 0:faces] = line
     pl.semaphore_wait(barrier, due)
+    send_ends(0, 0)
+    send_ends(0, 1)
     send_line(0, 0)
     send_near(0, (0, 1, 4, 5, 6, 7))
+    load_x.wait()
     column_pick = jnp.where(
         cols_iota((2 * side, cells)) == (rows_iota((2 * side, cells)) % side) * side
         + (rows_iota((2 * side, cells)) // side) * (side - 1), 1.0, 0.0).astype(BF16)
@@ -343,7 +346,11 @@
     send_line(0, 1)
     send_near(0, (2, 3))
     send_tails(0)
-    send_relay(0)
+
+    xp[:, 0] = zero_rows
+    xp[:, side + 1] = zero_rows
+    sp[:, 0] = zero_rows
+    sp[:, side + 1] = zero_rows
 
     load_w.wait()
     for a in range(3):
@@ -372,6 +379,7 @@
     def forward_face(f, carry):
         acc[pl.ds(pl.multiple_of(f * cells, cells), cells)] = conv(xp, f, wf[...]) + bias_ref[...]
         return carry
+    send_relay(0)
     lax.fori_loop(0, faces, forward_face, 0)
 
     def add_strip(edge, value):
@@ -452,6 +460,9 @@
         beyond.append(value)
         corner_src[1, 2 * v + h] = value.astype(BF16)
 
+    send_ends(1, 0)
+    send_ends(1, 1)
+
     @pl.when(rim)
     def _():
         for edge in range(4):
@@ -476,9 +487,8 @@
         @pl.when(jnp.logical_not(on_rim[edge]))
         def _(edge=edge):
             src[1, edge] = ring_strip(edge).astype(BF16).reshape(faces, side, width)
+    send_tails(1)
     send_near(1, range(8))
-    send_tails(1)
-    send_relay(1)
 
     def adjoint_face(f, carry):
         at = pl.ds(pl.multiple_of(f * cells, cells), cells)
@@ -488,7 +498,9 @@
         sp[f, 1:side + 1] = slope.astype(BF16).reshape(side, side, width)
         acc[at] = conv(sp, f, vf[...])
         return carry
-    lax.fori_loop(0, faces, adjoint_face, 0)
+    lax.fori_loop(0, faces // 3, adjoint_face, 0)
+    send_relay(1)
+    lax.fori_loop(faces // 3, faces, adjoint_face, 0)
 
     def adjoint_strip(edge):
         add_strip(edge, strip_in[1, edge].reshape(strip, width).astype(F32))
@@ -581,7 +593,7 @@
             dma((2,)),
             dma((2, 2, 2)),
             dma((2, 2, 2)),
-            dma((7,)),
+            dma((9,)),
         ],
         compiler_params=pltpu.CompilerParams(
             collective_id=0, has_side_effects=True, vmem_limit_bytes=40 * 1024 * 1024),

time: 41.8 us -> 41.7 us (level)
  no operation moved by 1% of the time
where the time goes in v4:
time: 41.7 us; the launch traced here: 41.6 us
  Pallas kernels  39.2 us (94%)
  local copies, waits for them, and re-layouts  1.76 us (4%)
  between operations  0.64 us (2%)
    pallas_call x1, Pallas kernels, shards(): pl.pallas_call(functools.partial(kernel, nx, ny, faces, side, width), out...  39.2 us
    unnamed x2, local copies, waits for them, and re-layouts  1.76 us

profile of v4, /device:TPU:57, one launch (start us, length us, event | category | flops | bytes accessed | tf_op | source)
XLA Modules:
  0.0 41.6 jit_solution(14033057088131921423)
XLA Ops:
  0.6 39.2 %shard_map.86 = (bf16[12,16,16,128]{3,2,1,0:T(8,128)(2,1)S(1)}, bf16[12,16,16,128]{3,2,1,0:T(8,128)(2,1)S(1)}) custom-call(s32[4,12]{1,0:T(4,128)} %bitcast.4, s32[4,12]{1,0:T(4,128)} %bitcast.5, s32[4,12]{1,0:T(4,128)} %bitcast.6, f32[1,128]{1,0:T(1,128)} %bitcast.7, bf16[12,16,16,128]{3,2,1,0:T(8,128)(2,1)} %x_hbm.1, bf16[3,3,128,128]{3,2,1,0:T(8,128)(2,1)} %w_hbm.1, ...), custom_call_target="tpu_custom_call" | custom-call | tf_op jit(solution)/shard_map/pallas_call | solution.py:558
  39.9 0.9 %copy.11 = bf16[12,16,16,128]{3,2,1,0:T(8,128)(2,1)} copy(bf16[12,16,16,128]{3,2,1,0:T(8,128)(2,1)S(1)} %get-tuple-element.4) | data formatting | bytes 1572864
  40.8 0.9 %copy.12 = bf16[12,16,16,128]{3,2,1,0:T(8,128)(2,1)} copy(bf16[12,16,16,128]{3,2,1,0:T(8,128)(2,1)S(1)} %get-tuple-element.5) | data formatting | bytes 1572864
